TPU v7x, 256 devices: a whole 4x4x8 slice. The times are simulated.
256 devices in a mesh: gx: 32 (over y_hi, z, core), gy: 8 (over x, y_lo).
Axes of the slice: x: 4, y: 4 (y_hi: 2, y_lo: 2; y = y_hi * 2 + y_lo), z: 8, core: 2. Of those that a mesh axis runs over, the one named last changes fastest.
Arguments:
- state: float32 [6, 2048, 4096], P(None, 'gx', 'gy'), may hold values from -1 to 1
- grade: int32 [2048, 4096], P('gx', 'gy'), may hold values from 0 to 15
- table: float32 [6, 16], replicated, may hold values from 0.02 to 1.5, as said below
Outputs:
- final_state: float32 [6, 2048, 4096], P(None, 'gx', 'gy')
Inputs may be any that keep to these rules, and one draw needn't show every extreme that they name: `table`: every entry is positive; row rate lies in 0.02 to 0.5, the others in 0.2 to 1.5.
All inputs are finite; a program needn't handle non-finite values.
Results may differ from a plain program's by a relative error of at most 0.0003.
Values sent between devices are 32-bit elements; how exact they have to be, the bound alone decides.
No kernel may reach another device: no remote copies, remote signals or barrier semaphores. Data moves between devices by JAX's collectives and lax.ppermute only.
A program may use at most 64 MiB of HBM per device.

v0:
```python
import jax
import jax.numpy as jnp
from jax import lax
from jax.sharding import PartitionSpec as P

STEPS = 8
SWEEPS = 3


DT = 0.2


def padded(cells, sides, width, closed):
    for axis, dim in sides:
        count = lax.axis_size(axis)
        ends = count if closed else count - 1
        head = lax.slice_in_dim(cells, 0, width, axis=dim)
        tail = lax.slice_in_dim(cells, cells.shape[dim] - width, cells.shape[dim], axis=dim)
        cells = jnp.concatenate(
            [
                lax.ppermute(tail, axis, [(i, (i + 1) % count) for i in range(ends)]),
                cells,
                lax.ppermute(head, axis, [((i + 1) % count, i) for i in range(ends)]),
            ],
            axis=dim,
        )
    return cells


def corner_mean(values):
    return 0.25 * (values[:-1, :-1] + values[1:, :-1] + values[:-1, 1:] + values[1:, 1:])


def advance(fields, params, ycol, ny):
    ux, uy, vx, vy, wx, wy = (fields[0], fields[1], fields[2], fields[3], fields[4], fields[5])
    lam, shear, beta, rinv, rate, eta = (
        params[0],
        params[1],
        params[2],
        params[3],
        params[4],
        params[5],
    )
    live = ((ycol >= 0) & (ycol < ny)).astype(jnp.float32)
    keep = live[:-1][None, :]
    exx = ux[1:, :-1] - ux[:-1, :-1]
    eyy = uy[:-1, 1:] - uy[:-1, :-1]
    exy = 0.5 * (ux[:-1, 1:] - ux[:-1, :-1] + (uy[1:, :-1] - uy[:-1, :-1]))
    lam_s = corner_mean(lam)
    mu_s = corner_mean(shear)
    beta_s = corner_mean(beta)
    trace = exx + eyy
    sxx = (lam_s * trace + 2.0 * mu_s * exx + beta_s * exx * exx * exx) * keep
    syy = (lam_s * trace + 2.0 * mu_s * eyy + beta_s * eyy * eyy * eyy) * keep
    sxy = (2.0 * mu_s * exy + beta_s * exy * exy * exy) * keep
    force_x = sxx[1:, 1:] - sxx[:-1, 1:] + (sxy[1:, 1:] - sxy[1:, :-1])
    force_y = sxy[1:, 1:] - sxy[:-1, 1:] + (syy[1:, 1:] - syy[1:, :-1])
    keep_c = live[1:-1][None, :]
    rinv_c = rinv[1:-1, 1:-1]
    rate_c = rate[1:-1, 1:-1]
    eta_c = eta[1:-1, 1:-1]
    wx_c = wx[1:-1, 1:-1]
    wy_c = wy[1:-1, 1:-1]
    new_vx = (vx[1:-1, 1:-1] + DT * rinv_c * (force_x - wx_c)) * keep_c
    new_vy = (vy[1:-1, 1:-1] + DT * rinv_c * (force_y - wy_c)) * keep_c
    new_wx = (wx_c + rate_c * (eta_c * force_x - wx_c)) * keep_c
    new_wy = (wy_c + rate_c * (eta_c * force_y - wy_c)) * keep_c
    new_ux = (ux[1:-1, 1:-1] + DT * new_vx) * keep_c
    new_uy = (uy[1:-1, 1:-1] + DT * new_vy) * keep_c
    return jnp.stack([new_ux, new_uy, new_vx, new_vy, new_wx, new_wy])


def shards(state, grade, table):
    rows_x = state.shape[1]
    cols_y = state.shape[2]
    total_y = cols_y * lax.axis_size("gy")
    first_col = lax.axis_index("gy") * cols_y
    grade_wide = padded(grade, (("gx", 0), ("gy", 1)), STEPS, True)
    levels = jnp.arange(table.shape[1], dtype=jnp.int32)
    onehot = (grade_wide[None, :, :] == levels[:, None, None]).astype(jnp.float32)
    params_wide = jnp.einsum("kg,gab->kab", table, onehot, precision=lax.Precision.HIGHEST)

    def columns(width):
        return first_col - width + jnp.arange(cols_y + 2 * width, dtype=jnp.int32)

    current = state
    for sweep in range(SWEEPS):
        for step in range(STEPS):
            offset = STEPS - 1
            wide = padded(current, (("gx", 1),), 1, True)
            wide = padded(wide, (("gy", 2),), 1, False)
            ycol = columns(1)
            live = ((ycol >= 0) & (ycol < total_y)).astype(jnp.float32)
            current = advance(
                wide * live[None, None, :],
                params_wide[:, offset : offset + rows_x + 2 * 1, offset : offset + cols_y + 2 * 1],
                columns(1),
                total_y,
            )
    return current


def solution(mesh):
    placed = (P(None, "gx", "gy"), P("gx", "gy"), P())
    return jax.shard_map(
        shards, mesh=mesh, in_specs=placed, out_specs=P(None, "gx", "gy"), check_vma=False
    )
```

profile of v0, /device:TPU:8, one launch (start us, length us, event | category | flops | bytes accessed | tf_op | source)
XLA Modules:
  0.0 682.8 jit_solution(13152569016972221946)
XLA Ops:
  1.1 7.1 %collective-permute-start.1 = (f32[6,1,512]{2,1,0:T(1,128)S(1)}, f32[6,1,512]{2,1,0:T(1,128)S(1)}, u32[]{:S(2)}, u32[]{:S(2)}) collective-permute-start(f32[6,1,512]{2,1,0:T(1,128)S(1)} %get-tuple-element.444), channel_id=1, source_target_pairs={{8,0},{16,8},{24,16},{32,24},{40,32},{48,40},{56,48},{64,56},{72,6... | collective-permute-start | bytes 36872 | tf_op jit(solution)/shard_map/ppermute | solution.py:23
  41.6 5.6 collective-permute-start.9
  68.9 5.3 collective-permute-start.13
  97.1 5.3 collective-permute-start.17
  152.0 5.3 collective-permute-start.25
  179.1 5.3 collective-permute-start.29
  192.9 6.3 collective-permute-done.30
  207.2 5.3 collective-permute-start.33
  221.2 6.1 collective-permute-done.34
  235.4 5.3 collective-permute-start.37
  249.2 6.3 collective-permute-done.38
  263.5 5.3 collective-permute-start.41
  277.3 6.3 collective-permute-done.42
  305.7 6.1 collective-permute-done.46
  319.8 5.3 collective-permute-start.49
  333.6 6.3 collective-permute-done.50
  348.0 5.3 collective-permute-start.53
  361.8 6.3 collective-permute-done.54
  376.1 5.3 collective-permute-start.57
  390.3 5.9 collective-permute-done.58
  418.1 6.3 collective-permute-done.62
  446.2 6.3 collective-permute-done.66
  474.6 6.2 collective-permute-done.70
  502.6 6.3 collective-permute-done.74
  516.9 5.3 collective-permute-start.77
  530.7 6.3 collective-permute-done.78
  545.1 5.3 collective-permute-start.81
  559.1 6.1 collective-permute-done.82
  587.0 6.3 collective-permute-done.86
  615.1 6.3 collective-permute-done.90
  643.5 6.1 collective-permute-done.94
  671.4 6.3 collective-permute-done.98
  (458 shorter events, 491.4 us)
Async XLA Ops:
  9.0 16.3 %collective-permute-start.5 = (s32[8,512]{1,0:T(8,128)S(1)}, s32[8,512]{1,0:T(8,128)S(1)}, u32[]{:S(2)}, u32[]{:S(2)}) collective-permute-start(s32[8,512]{1,0:T(8,128)S(1)} %get-tuple-element.472), channel_id=1, source_target_pairs={{8,0},{16,8},{24,16},{32,24},{40,32},{48,40},{56,48},{64,56},{72,6... | collective-permute-start | bytes 49160 | tf_op jit(solution)/shard_map/ppermute | solution.py:23
  9.6 15.6 %collective-permute-start.4 = (s32[8,512]{1,0:T(8,128)S(1)}, s32[8,512]{1,0:T(8,128)S(1)}, u32[]{:S(2)}, u32[]{:S(2)}) collective-permute-start(s32[8,512]{1,0:T(8,128)S(1)} %get-tuple-element.473), channel_id=1, source_target_pairs={{0,8},{8,16},{16,24},{24,32},{32,40},{40,48},{48,56},{56,64},{64,7... | collective-permute-start | bytes 49160 | tf_op jit(solution)/shard_map/ppermute | solution.py:21
  15.0 9.7 %collective-permute-start.3 = (f32[6,66,1]{2,1,0:T(8,128)S(1)}, f32[6,66,1]{2,1,0:T(8,128)S(1)}, u32[]{:S(2)}, u32[]{:S(2)}) collective-permute-start(f32[6,66,1]{2,1,0:T(8,128)S(1)} %get-tuple-element.396), channel_id=1, source_target_pairs={{1,0},{2,1},{3,2},{4,3},{5,4},{6,5},{7,6},{9,8},{10,9},{11,10},{12... | collective-permute-start | bytes 4760 | tf_op jit(solution)/shard_map/ppermute | solution.py:23
  187.1 12.2 %collective-permute-start.30 = (f32[6,66,1]{2,1,0:T(8,128)S(1)}, f32[6,66,1]{2,1,0:T(8,128)S(1)}, u32[]{:S(2)}, u32[]{:S(2)}) collective-permute-start(f32[6,66,1]{2,1,0:T(8,128)S(1)} %get-tuple-element.383), channel_id=1, source_target_pairs={{0,1},{1,2},{2,3},{3,4},{4,5},{5,6},{6,7},{8,9},{9,10},{10,11},{11... | collective-permute-start | bytes 4760 | tf_op jit(solution)/shard_map/ppermute | solution.py:21
  215.2 12.2 %collective-permute-start.34 = (f32[6,66,1]{2,1,0:T(8,128)S(1)}, f32[6,66,1]{2,1,0:T(8,128)S(1)}, u32[]{:S(2)}, u32[]{:S(2)}) collective-permute-start(f32[6,66,1]{2,1,0:T(8,128)S(1)} %get-tuple-element.381), channel_id=1, source_target_pairs={{0,1},{1,2},{2,3},{3,4},{4,5},{5,6},{6,7},{8,9},{9,10},{10,11},{11... | collective-permute-start | bytes 4760 | tf_op jit(solution)/shard_map/ppermute | solution.py:21
  243.3 12.2 %collective-permute-start.38 = (f32[6,66,1]{2,1,0:T(8,128)S(1)}, f32[6,66,1]{2,1,0:T(8,128)S(1)}, u32[]{:S(2)}, u32[]{:S(2)}) collective-permute-start(f32[6,66,1]{2,1,0:T(8,128)S(1)} %get-tuple-element.379), channel_id=1, source_target_pairs={{0,1},{1,2},{2,3},{3,4},{4,5},{5,6},{6,7},{8,9},{9,10},{10,11},{11... | collective-permute-start | bytes 4760 | tf_op jit(solution)/shard_map/ppermute | solution.py:21
  246.0 9.5 %collective-permute-start.39 = (f32[6,66,1]{2,1,0:T(8,128)S(1)}, f32[6,66,1]{2,1,0:T(8,128)S(1)}, u32[]{:S(2)}, u32[]{:S(2)}) collective-permute-start(f32[6,66,1]{2,1,0:T(8,128)S(1)} %get-tuple-element.380), channel_id=1, source_target_pairs={{1,0},{2,1},{3,2},{4,3},{5,4},{6,5},{7,6},{9,8},{10,9},{11,10},{12... | collective-permute-start | bytes 4760 | tf_op jit(solution)/shard_map/ppermute | solution.py:23
  271.4 12.2 %collective-permute-start.42 = (f32[6,66,1]{2,1,0:T(8,128)S(1)}, f32[6,66,1]{2,1,0:T(8,128)S(1)}, u32[]{:S(2)}, u32[]{:S(2)}) collective-permute-start(f32[6,66,1]{2,1,0:T(8,128)S(1)} %get-tuple-element.377), channel_id=1, source_target_pairs={{0,1},{1,2},{2,3},{3,4},{4,5},{5,6},{6,7},{8,9},{9,10},{10,11},{11... | collective-permute-start | bytes 4760 | tf_op jit(solution)/shard_map/ppermute | solution.py:21
  274.1 9.6 %collective-permute-start.43 = (f32[6,66,1]{2,1,0:T(8,128)S(1)}, f32[6,66,1]{2,1,0:T(8,128)S(1)}, u32[]{:S(2)}, u32[]{:S(2)}) collective-permute-start(f32[6,66,1]{2,1,0:T(8,128)S(1)} %get-tuple-element.378), channel_id=1, source_target_pairs={{1,0},{2,1},{3,2},{4,3},{5,4},{6,5},{7,6},{9,8},{10,9},{11,10},{12... | collective-permute-start | bytes 4760 | tf_op jit(solution)/shard_map/ppermute | solution.py:23
  299.6 12.2 %collective-permute-start.46 = (f32[6,66,1]{2,1,0:T(8,128)S(1)}, f32[6,66,1]{2,1,0:T(8,128)S(1)}, u32[]{:S(2)}, u32[]{:S(2)}) collective-permute-start(f32[6,66,1]{2,1,0:T(8,128)S(1)} %get-tuple-element.375), channel_id=1, source_target_pairs={{0,1},{1,2},{2,3},{3,4},{4,5},{5,6},{6,7},{8,9},{9,10},{10,11},{11... | collective-permute-start | bytes 4760 | tf_op jit(solution)/shard_map/ppermute | solution.py:21
  302.2 9.6 %collective-permute-start.47 = (f32[6,66,1]{2,1,0:T(8,128)S(1)}, f32[6,66,1]{2,1,0:T(8,128)S(1)}, u32[]{:S(2)}, u32[]{:S(2)}) collective-permute-start(f32[6,66,1]{2,1,0:T(8,128)S(1)} %get-tuple-element.376), channel_id=1, source_target_pairs={{1,0},{2,1},{3,2},{4,3},{5,4},{6,5},{7,6},{9,8},{10,9},{11,10},{12... | collective-permute-start | bytes 4760 | tf_op jit(solution)/shard_map/ppermute | solution.py:23
  327.7 12.2 %collective-permute-start.50 = (f32[6,66,1]{2,1,0:T(8,128)S(1)}, f32[6,66,1]{2,1,0:T(8,128)S(1)}, u32[]{:S(2)}, u32[]{:S(2)}) collective-permute-start(f32[6,66,1]{2,1,0:T(8,128)S(1)} %get-tuple-element.373), channel_id=1, source_target_pairs={{0,1},{1,2},{2,3},{3,4},{4,5},{5,6},{6,7},{8,9},{9,10},{10,11},{11... | collective-permute-start | bytes 4760 | tf_op jit(solution)/shard_map/ppermute | solution.py:21
  330.4 9.6 %collective-permute-start.51 = (f32[6,66,1]{2,1,0:T(8,128)S(1)}, f32[6,66,1]{2,1,0:T(8,128)S(1)}, u32[]{:S(2)}, u32[]{:S(2)}) collective-permute-start(f32[6,66,1]{2,1,0:T(8,128)S(1)} %get-tuple-element.374), channel_id=1, source_target_pairs={{1,0},{2,1},{3,2},{4,3},{5,4},{6,5},{7,6},{9,8},{10,9},{11,10},{12... | collective-permute-start | bytes 4760 | tf_op jit(solution)/shard_map/ppermute | solution.py:23
  355.9 12.2 %collective-permute-start.54 = (f32[6,66,1]{2,1,0:T(8,128)S(1)}, f32[6,66,1]{2,1,0:T(8,128)S(1)}, u32[]{:S(2)}, u32[]{:S(2)}) collective-permute-start(f32[6,66,1]{2,1,0:T(8,128)S(1)} %get-tuple-element.371), channel_id=1, source_target_pairs={{0,1},{1,2},{2,3},{3,4},{4,5},{5,6},{6,7},{8,9},{9,10},{10,11},{11... | collective-permute-start | bytes 4760 | tf_op jit(solution)/shard_map/ppermute | solution.py:21
  358.5 9.6 %collective-permute-start.55 = (f32[6,66,1]{2,1,0:T(8,128)S(1)}, f32[6,66,1]{2,1,0:T(8,128)S(1)}, u32[]{:S(2)}, u32[]{:S(2)}) collective-permute-start(f32[6,66,1]{2,1,0:T(8,128)S(1)} %get-tuple-element.372), channel_id=1, source_target_pairs={{1,0},{2,1},{3,2},{4,3},{5,4},{6,5},{7,6},{9,8},{10,9},{11,10},{12... | collective-permute-start | bytes 4760 | tf_op jit(solution)/shard_map/ppermute | solution.py:23
  384.1 12.2 %collective-permute-start.58 = (f32[6,66,1]{2,1,0:T(8,128)S(1)}, f32[6,66,1]{2,1,0:T(8,128)S(1)}, u32[]{:S(2)}, u32[]{:S(2)}) collective-permute-start(f32[6,66,1]{2,1,0:T(8,128)S(1)} %get-tuple-element.369), channel_id=1, source_target_pairs={{0,1},{1,2},{2,3},{3,4},{4,5},{5,6},{6,7},{8,9},{9,10},{10,11},{11... | collective-permute-start | bytes 4760 | tf_op jit(solution)/shard_map/ppermute | solution.py:21
  386.7 9.6 %collective-permute-start.59 = (f32[6,66,1]{2,1,0:T(8,128)S(1)}, f32[6,66,1]{2,1,0:T(8,128)S(1)}, u32[]{:S(2)}, u32[]{:S(2)}) collective-permute-start(f32[6,66,1]{2,1,0:T(8,128)S(1)} %get-tuple-element.370), channel_id=1, source_target_pairs={{1,0},{2,1},{3,2},{4,3},{5,4},{6,5},{7,6},{9,8},{10,9},{11,10},{12... | collective-permute-start | bytes 4760 | tf_op jit(solution)/shard_map/ppermute | solution.py:23
  412.2 12.2 %collective-permute-start.62 = (f32[6,66,1]{2,1,0:T(8,128)S(1)}, f32[6,66,1]{2,1,0:T(8,128)S(1)}, u32[]{:S(2)}, u32[]{:S(2)}) collective-permute-start(f32[6,66,1]{2,1,0:T(8,128)S(1)} %get-tuple-element.367), channel_id=1, source_target_pairs={{0,1},{1,2},{2,3},{3,4},{4,5},{5,6},{6,7},{8,9},{9,10},{10,11},{11... | collective-permute-start | bytes 4760 | tf_op jit(solution)/shard_map/ppermute | solution.py:21
  414.9 9.6 %collective-permute-start.63 = (f32[6,66,1]{2,1,0:T(8,128)S(1)}, f32[6,66,1]{2,1,0:T(8,128)S(1)}, u32[]{:S(2)}, u32[]{:S(2)}) collective-permute-start(f32[6,66,1]{2,1,0:T(8,128)S(1)} %get-tuple-element.368), channel_id=1, source_target_pairs={{1,0},{2,1},{3,2},{4,3},{5,4},{6,5},{7,6},{9,8},{10,9},{11,10},{12... | collective-permute-start | bytes 4760 | tf_op jit(solution)/shard_map/ppermute | solution.py:23
  440.4 12.2 %collective-permute-start.66 = (f32[6,66,1]{2,1,0:T(8,128)S(1)}, f32[6,66,1]{2,1,0:T(8,128)S(1)}, u32[]{:S(2)}, u32[]{:S(2)}) collective-permute-start(f32[6,66,1]{2,1,0:T(8,128)S(1)} %get-tuple-element.365), channel_id=1, source_target_pairs={{0,1},{1,2},{2,3},{3,4},{4,5},{5,6},{6,7},{8,9},{9,10},{10,11},{11... | collective-permute-start | bytes 4760 | tf_op jit(solution)/shard_map/ppermute | solution.py:21
  443.0 9.6 %collective-permute-start.67 = (f32[6,66,1]{2,1,0:T(8,128)S(1)}, f32[6,66,1]{2,1,0:T(8,128)S(1)}, u32[]{:S(2)}, u32[]{:S(2)}) collective-permute-start(f32[6,66,1]{2,1,0:T(8,128)S(1)} %get-tuple-element.366), channel_id=1, source_target_pairs={{1,0},{2,1},{3,2},{4,3},{5,4},{6,5},{7,6},{9,8},{10,9},{11,10},{12... | collective-permute-start | bytes 4760 | tf_op jit(solution)/shard_map/ppermute | solution.py:23
  468.5 12.2 %collective-permute-start.70 = (f32[6,66,1]{2,1,0:T(8,128)S(1)}, f32[6,66,1]{2,1,0:T(8,128)S(1)}, u32[]{:S(2)}, u32[]{:S(2)}) collective-permute-start(f32[6,66,1]{2,1,0:T(8,128)S(1)} %get-tuple-element.363), channel_id=1, source_target_pairs={{0,1},{1,2},{2,3},{3,4},{4,5},{5,6},{6,7},{8,9},{9,10},{10,11},{11... | collective-permute-start | bytes 4760 | tf_op jit(solution)/shard_map/ppermute | solution.py:21
  471.2 9.6 %collective-permute-start.71 = (f32[6,66,1]{2,1,0:T(8,128)S(1)}, f32[6,66,1]{2,1,0:T(8,128)S(1)}, u32[]{:S(2)}, u32[]{:S(2)}) collective-permute-start(f32[6,66,1]{2,1,0:T(8,128)S(1)} %get-tuple-element.364), channel_id=1, source_target_pairs={{1,0},{2,1},{3,2},{4,3},{5,4},{6,5},{7,6},{9,8},{10,9},{11,10},{12... | collective-permute-start | bytes 4760 | tf_op jit(solution)/shard_map/ppermute | solution.py:23
  496.7 12.2 %collective-permute-start.74 = (f32[6,66,1]{2,1,0:T(8,128)S(1)}, f32[6,66,1]{2,1,0:T(8,128)S(1)}, u32[]{:S(2)}, u32[]{:S(2)}) collective-permute-start(f32[6,66,1]{2,1,0:T(8,128)S(1)} %get-tuple-element.361), channel_id=1, source_target_pairs={{0,1},{1,2},{2,3},{3,4},{4,5},{5,6},{6,7},{8,9},{9,10},{10,11},{11... | collective-permute-start | bytes 4760 | tf_op jit(solution)/shard_map/ppermute | solution.py:21
  499.4 9.6 %collective-permute-start.75 = (f32[6,66,1]{2,1,0:T(8,128)S(1)}, f32[6,66,1]{2,1,0:T(8,128)S(1)}, u32[]{:S(2)}, u32[]{:S(2)}) collective-permute-start(f32[6,66,1]{2,1,0:T(8,128)S(1)} %get-tuple-element.362), channel_id=1, source_target_pairs={{1,0},{2,1},{3,2},{4,3},{5,4},{6,5},{7,6},{9,8},{10,9},{11,10},{12... | collective-permute-start | bytes 4760 | tf_op jit(solution)/shard_map/ppermute | solution.py:23
  524.9 12.2 %collective-permute-start.78 = (f32[6,66,1]{2,1,0:T(8,128)S(1)}, f32[6,66,1]{2,1,0:T(8,128)S(1)}, u32[]{:S(2)}, u32[]{:S(2)}) collective-permute-start(f32[6,66,1]{2,1,0:T(8,128)S(1)} %get-tuple-element.359), channel_id=1, source_target_pairs={{0,1},{1,2},{2,3},{3,4},{4,5},{5,6},{6,7},{8,9},{9,10},{10,11},{11... | collective-permute-start | bytes 4760 | tf_op jit(solution)/shard_map/ppermute | solution.py:21
  527.5 9.6 %collective-permute-start.79 = (f32[6,66,1]{2,1,0:T(8,128)S(1)}, f32[6,66,1]{2,1,0:T(8,128)S(1)}, u32[]{:S(2)}, u32[]{:S(2)}) collective-permute-start(f32[6,66,1]{2,1,0:T(8,128)S(1)} %get-tuple-element.360), channel_id=1, source_target_pairs={{1,0},{2,1},{3,2},{4,3},{5,4},{6,5},{7,6},{9,8},{10,9},{11,10},{12... | collective-permute-start | bytes 4760 | tf_op jit(solution)/shard_map/ppermute | solution.py:23
  553.0 12.2 %collective-permute-start.82 = (f32[6,66,1]{2,1,0:T(8,128)S(1)}, f32[6,66,1]{2,1,0:T(8,128)S(1)}, u32[]{:S(2)}, u32[]{:S(2)}) collective-permute-start(f32[6,66,1]{2,1,0:T(8,128)S(1)} %get-tuple-element.357), channel_id=1, source_target_pairs={{0,1},{1,2},{2,3},{3,4},{4,5},{5,6},{6,7},{8,9},{9,10},{10,11},{11... | collective-permute-start | bytes 4760 | tf_op jit(solution)/shard_map/ppermute | solution.py:21
  581.1 12.2 %collective-permute-start.86 = (f32[6,66,1]{2,1,0:T(8,128)S(1)}, f32[6,66,1]{2,1,0:T(8,128)S(1)}, u32[]{:S(2)}, u32[]{:S(2)}) collective-permute-start(f32[6,66,1]{2,1,0:T(8,128)S(1)} %get-tuple-element.355), channel_id=1, source_target_pairs={{0,1},{1,2},{2,3},{3,4},{4,5},{5,6},{6,7},{8,9},{9,10},{10,11},{11... | collective-permute-start | bytes 4760 | tf_op jit(solution)/shard_map/ppermute | solution.py:21
  609.3 12.2 %collective-permute-start.90 = (f32[6,66,1]{2,1,0:T(8,128)S(1)}, f32[6,66,1]{2,1,0:T(8,128)S(1)}, u32[]{:S(2)}, u32[]{:S(2)}) collective-permute-start(f32[6,66,1]{2,1,0:T(8,128)S(1)} %get-tuple-element.353), channel_id=1, source_target_pairs={{0,1},{1,2},{2,3},{3,4},{4,5},{5,6},{6,7},{8,9},{9,10},{10,11},{11... | collective-permute-start | bytes 4760 | tf_op jit(solution)/shard_map/ppermute | solution.py:21
  637.4 12.2 %collective-permute-start.94 = (f32[6,66,1]{2,1,0:T(8,128)S(1)}, f32[6,66,1]{2,1,0:T(8,128)S(1)}, u32[]{:S(2)}, u32[]{:S(2)}) collective-permute-start(f32[6,66,1]{2,1,0:T(8,128)S(1)} %get-tuple-element.351), channel_id=1, source_target_pairs={{0,1},{1,2},{2,3},{3,4},{4,5},{5,6},{6,7},{8,9},{9,10},{10,11},{11... | collective-permute-start | bytes 4760 | tf_op jit(solution)/shard_map/ppermute | solution.py:21
  665.5 12.2 %collective-permute-start.98 = (f32[6,66,1]{2,1,0:T(8,128)S(1)}, f32[6,66,1]{2,1,0:T(8,128)S(1)}, u32[]{:S(2)}, u32[]{:S(2)}) collective-permute-start(f32[6,66,1]{2,1,0:T(8,128)S(1)} %get-tuple-element.349), channel_id=1, source_target_pairs={{0,1},{1,2},{2,3},{3,4},{4,5},{5,6},{6,7},{8,9},{9,10},{10,11},{11... | collective-permute-start | bytes 4760 | tf_op jit(solution)/shard_map/ppermute | solution.py:21
  (74 other events, 570.1 us)
where the time goes:
time: 695 us; the launch traced here: 683 us
  starting transfers between devices  279 us (40%)
  waiting for transfers between devices  185 us (27%)
  other arithmetic  156 us (22%)
  local copies, waits for them, and re-layouts  59.5 us (9%)
    ppermute x50, starting transfers between devices, padded(): lax.ppermute(head, axis, [((i + 1) % count, i) for i in range(ends)])  208 us
    ppermute x50, waiting for transfers between devices, padded(): lax.ppermute(tail, axis, [(i, (i + 1) % count) for i in range(ends)])  160 us
    ppermute x50, starting transfers between devices, padded(): lax.ppermute(tail, axis, [(i, (i + 1) % count) for i in range(ends)])  70.6 us
    unnamed x72, other arithmetic  63.2 us
    mul x24, other arithmetic, shards(): wide * live[None, None, :]  38 us
    unnamed x62, local copies, waits for them, and re-layouts  31 us
    slice x24, other arithmetic, padded(): lax.slice_in_dim(cells, cells.shape[dim] - width, cells.shape[dim], axis=...  28.2 us
    ppermute x50, waiting for transfers between devices, padded(): lax.ppermute(head, axis, [((i + 1) % count, i) for i in range(ends)])  25.5 us
  transfers between devices with their start and end apart: 100, of which 56 were waited for; matrix products, arithmetic and copies ran while one was open for 0% of the time, Pallas kernels for 0%

commit v1 on v0

v1 whole, which is shorter than its diff:
```python
import functools

import jax
import jax.numpy as jnp
from jax import lax
from jax.experimental import pallas as pl
from jax.experimental.pallas import tpu as pltpu
from jax.sharding import PartitionSpec as P

STEPS = 24
DT = 0.2
F32 = jnp.float32
H = 24
CT = 5
EDGE = 4
PACK = 4

VMEM = pl.BlockSpec(memory_space=pltpu.VMEM)
SMEM = pl.BlockSpec(memory_space=pltpu.SMEM)


def lanes():
    return lax.broadcasted_iota(jnp.int32, (8, 128), 1)


def sublanes():
    return lax.broadcasted_iota(jnp.int32, (8, 128), 0)


def edge_live(gy, count, width):
    right = jnp.where(gy < count - 1, 1, 0)
    left = jnp.where(gy > 0, 1, 0)
    return jnp.where(lanes() < 64, right, left) > 0


def pack_y_kernel(state_ref, grade_ref, left_ref, right_ref):
    rows = state_ref.shape[1]
    group = rows // PACK
    lane = lanes()

    def read(field, row, col):
        if field < 6:
            return state_ref[field, row : row + 8, col : col + 128]
        return grade_ref[row : row + 8, col : col + 128].astype(F32)

    last = state_ref.shape[2] - 128
    for field in range(7):
        for k in range(group // 8):
            to_left = None
            to_right = None
            for q in range(PACK):
                row = q * group + 8 * k
                a = read(field, row, 0)
                b = read(field, row, last)
                if q:
                    a = pltpu.roll(a, 32 * q, 1)
                b = pltpu.roll(b, 32 * q + H, 1)
                here = lane >= 32 * q
                to_left = a if q == 0 else jnp.where(here, a, to_left)
                to_right = b if q == 0 else jnp.where(here, b, to_right)
            left_ref[field, 8 * k : 8 * k + 8, :] = to_left
            right_ref[field, 8 * k : 8 * k + 8, :] = to_right


def pack_x_kernel(count, gy_ref, state_ref, grade_ref, from_left_ref, from_right_ref, edge_ref, up_ref, down_ref):
    rows = state_ref.shape[1]
    group = rows // PACK
    lane = lanes()
    live = edge_live(gy_ref[0], count, state_ref.shape[2])
    for field in range(7):
        for k in range(group // 8):
            right = from_right_ref[field, 8 * k : 8 * k + 8, :]
            left = from_left_ref[field, 8 * k : 8 * k + 8, :]
            for q in range(PACK):
                r = right if q == 0 else pltpu.roll(right, 128 - 32 * q, 1)
                s = pltpu.roll(left, (128 - H - 32 * q) % 128, 1)
                both = jnp.where(lane < H, r, jnp.where(lane >= 128 - H, s, 0.0))
                if field < 6:
                    both = jnp.where(live, both, 0.0)
                row = q * group + 8 * k
                edge_ref[field, row : row + 8, :] = both
                if row < H:
                    up_ref[field, EDGE, row : row + 8, :] = both
                if row >= rows - H:
                    down_ref[field, EDGE, row - rows + H : row - rows + H + 8, :] = both
    for field in range(7):
        for c in range(CT - 1):
            cols = slice(128 * c, 128 * c + 128)
            if field < 6:
                up_ref[field, c] = state_ref[field, 0:H, cols]
                down_ref[field, c] = state_ref[field, rows - H : rows, cols]
            else:
                up_ref[field, c] = grade_ref[0:H, cols].astype(F32)
                down_ref[field, c] = grade_ref[rows - H : rows, cols].astype(F32)


def tables(table_ref, tab):
    tab[0:6, 0:16] = table_ref[...]

    def row(q):
        return jnp.broadcast_to(tab[q : q + 1, :], (8, 128))

    rate = row(4)
    return (
        0.25 * row(0),
        0.25 * row(1),
        0.25 * row(2),
        (DT * DT) * row(3),
        1.0 - rate,
        rate * row(5),
    )


def look_up(tabs, grade):
    return [jnp.take_along_axis(t, grade, axis=1) for t in tabs]


def put_raw(pr, tabs, live, grade_of, tiles, first_row):
    for k in range(tiles):
        for c in range(CT):
            lam, mu, beta, dr, om, re = look_up(tabs, grade_of(c, k))
            if c == EDGE:
                dr = jnp.where(live, dr, 0.0)
                re = jnp.where(live, re, 0.0)
            where = (c, pl.ds(first_row + 8 * k, 8), slice(None))
            pr[(0,) + where] = lam
            pr[(1,) + where] = mu
            pr[(3,) + where] = beta
            pr[(5,) + where] = dr
            pr[(6,) + where] = om
            pr[(7,) + where] = re


def put_means(pr, live, tiles):
    last = lanes() == 127
    for k in range(tiles):
        for q in (0, 1, 3):
            sums = [pr[q, c, pl.ds(8 * k, 8), :] + pr[q, c, pl.ds(8 * k + 1, 8), :] for c in range(CT)]
            moved = following(sums, last)
            for c in range(CT):
                mean = sums[c] + moved[c]
                if c == EDGE:
                    mean = jnp.where(live, mean, 0.0)
                where = (c, pl.ds(8 * k, 8), slice(None))
                if q == 0:
                    pr[(0,) + where] = mean
                elif q == 1:
                    pr[(1,) + where] = 2.0 * mean
                    pr[(2,) + where] = mean
                else:
                    pr[(3,) + where] = mean
                    pr[(4,) + where] = 0.125 * mean


def following(tiles, last):
    rolled = [pltpu.roll(x, 127, 1) for x in tiles]
    return [jnp.where(last, rolled[(c + 1) % CT], rolled[c]) for c in range(CT)]


def preceding(tiles, first):
    rolled = [pltpu.roll(x, 1, 1) for x in tiles]
    return [jnp.where(first, rolled[(c - 1) % CT], rolled[c]) for c in range(CT)]


def read(ref, plane, rows):
    return [ref[plane, c, rows, :] for c in range(CT)]


def stresses(pr, rows, ux, uy, uxn, uyn):
    lane = lanes()
    last = lane == 127
    first = lane == 0
    uxr = following(ux, last)
    uyr = following(uy, last)
    lam, mu2, mu, beta, beta8 = [read(pr, q, rows) for q in range(5)]
    sxx, sxy, syy = [], [], []
    for c in range(CT):
        exx = uxn[c] - ux[c]
        eyy = uyr[c] - uy[c]
        g = (uxr[c] - ux[c]) + (uyn[c] - uy[c])
        trace = lam[c] * (exx + eyy)
        sxx.append(trace + exx * (mu2[c] + beta[c] * (exx * exx)))
        syy.append(trace + eyy * (mu2[c] + beta[c] * (eyy * eyy)))
        sxy.append(g * (mu[c] + beta8[c] * (g * g)))
    sxy_l = preceding(sxy, first)
    syy_l = preceding(syy, first)
    gx = [sxx[c] + (sxy[c] - sxy_l[c]) for c in range(CT)]
    gy = [sxy[c] + (syy[c] - syy_l[c]) for c in range(CT)]
    return gx, gy, sxx, sxy


def update(st, pr, rows, ux, uy, gx, gy, px, py):
    dr, om, re = [read(pr, q, rows) for q in (5, 6, 7)]
    vx, vy, wx, wy = [read(st, q, rows) for q in (2, 3, 4, 5)]
    for c in range(CT):
        fx = gx[c] - px[c]
        fy = gy[c] - py[c]
        new_vx = vx[c] + dr[c] * (fx - wx[c])
        new_vy = vy[c] + dr[c] * (fy - wy[c])
        st[2, c, rows, :] = new_vx
        st[3, c, rows, :] = new_vy
        st[4, c, rows, :] = om[c] * wx[c] + re[c] * fx
        st[5, c, rows, :] = om[c] * wy[c] + re[c] * fy
        st[0, c, rows, :] = ux[c] + new_vx
        st[1, c, rows, :] = uy[c] + new_vy


def interior_kernel(count, gy_ref, table_ref, state_ref, grade_ref, edge_ref, keep_ref, tail_ref, trace_ref, st, pr, ss, tab):
    rows = state_ref.shape[1]
    live = edge_live(gy_ref[0], count, state_ref.shape[2])
    tabs = tables(table_ref, tab)

    def grade_of(c, k):
        if c == EDGE:
            return edge_ref[6, 8 * k : 8 * k + 8, :].astype(jnp.int32)
        return grade_ref[8 * k : 8 * k + 8, 128 * c : 128 * c + 128]

    put_raw(pr, tabs, live, grade_of, rows // 8, 0)
    put_means(pr, live, rows // 8)
    for f in range(6):
        for c in range(CT):
            block = edge_ref[f] if c == EDGE else state_ref[f, :, 128 * c : 128 * c + 128]
            if f in (2, 3):
                block = DT * block
            st[f, c, 0:rows, :] = block
            tail_ref[f, c, H - 1 : H, :] = block[rows - 1 : rows]

    for g in range(STEPS // 4):
        n = rows // 8 - g

        def body(k, carry, n=n, g=g):
            base = 4 * g + k

            def at(offset):
                return pl.ds(base + offset, 8, stride=n)

            ux, uy = read(st, 0, at(0)), read(st, 1, at(0))
            uxn, uyn = read(st, 0, at(1)), read(st, 1, at(1))
            gx0, gy0, px, py = stresses(pr, at(0), ux, uy, uxn, uyn)
            for c in range(CT):
                trace_ref[0, c, pl.ds(base, 1), :] = gx0[c][0:1]
                trace_ref[1, c, pl.ds(base, 1), :] = gy0[c][0:1]
            for r in range(n):
                ux, uy = uxn, uyn
                for c in range(CT):
                    ss[0, c, at(r), :] = px[c]
                    ss[1, c, at(r), :] = py[c]
                if r < n - 1:
                    uxn, uyn = read(st, 0, at(r + 2)), read(st, 1, at(r + 2))
                    gx, gy, qx, qy = stresses(pr, at(r + 1), ux, uy, uxn, uyn)
                else:
                    gx = [pltpu.roll(v, 7, 0) for v in gx0]
                    gy = [pltpu.roll(v, 7, 0) for v in gy0]
                    qx, qy = px, py
                update(st, pr, at(r + 1), ux, uy, gx, gy, px, py)
                px, py = qx, qy
            row = rows - 2 - base
            for c in range(CT):
                for q in range(2):
                    trace_ref[2 + q, c, pl.ds(base, 1), :] = ss[q, c, pl.ds(row, 1), :]

                @pl.when(base < STEPS - 1)
                def _():
                    for f in range(6):
                        tail_ref[f, c, pl.ds(H - 2 - base, 1), :] = st[f, c, pl.ds(row, 1), :]

            return carry

        lax.fori_loop(0, 4, body, 0)
    for f in range(6):
        for c in range(CT):
            keep_ref[f, c] = st[f, c, 0 : rows - H, :]


def exterior_kernel(
    count, gy_ref, table_ref, grade_ref, edge_ref, keep_ref, tail_ref, trace_ref, top_ref, bottom_ref, out_ref, sa, pa, sb, pb, tab
):
    rows = grade_ref.shape[0]
    live = edge_live(gy_ref[0], count, grade_ref.shape[1])
    tabs = tables(table_ref, tab)
    near = H // 8

    def grades(first, halo_ref):
        def grade_of(c, k):
            if halo_ref is not None:
                return halo_ref[6, c, 8 * k : 8 * k + 8, :].astype(jnp.int32)
            row = first + 8 * k
            if c == EDGE:
                return edge_ref[6, row : row + 8, :].astype(jnp.int32)
            return grade_ref[row : row + 8, 128 * c : 128 * c + 128]

        return grade_of

    put_raw(pa, tabs, live, grades(0, top_ref), near, 0)
    put_raw(pa, tabs, live, grades(0, None), near, H)
    put_raw(pb, tabs, live, grades(rows - H, None), near, 0)
    put_raw(pb, tabs, live, grades(0, bottom_ref), near, H)
    put_means(pa, live, 2 * near)
    put_means(pb, live, 2 * near)
    for f in range(6):
        for c in range(CT):
            top = top_ref[f, c]
            bottom = bottom_ref[f, c]
            if f in (2, 3):
                top = DT * top
                bottom = DT * bottom
            sa[f, c, 0:H, :] = top
            sa[f, c, H : 2 * H, :] = keep_ref[f, c, 0:H, :]
            sb[f, c, 0:H, :] = tail_ref[f, c]
            sb[f, c, H : 2 * H, :] = bottom

    sub = sublanes()
    n = near

    def body(base, carry):
        def at(offset):
            return pl.ds(base + offset, 8, stride=n)

        def bt(offset):
            return pl.ds(H - 1 - base + offset, 8, stride=n)

        def trace(q):
            return [jnp.broadcast_to(trace_ref[q, c, pl.ds(base, 1), :], (8, 128)) for c in range(CT)]

        ux, uy = read(sa, 0, at(0)), read(sa, 1, at(0))
        uxn, uyn = read(sa, 0, at(1)), read(sa, 1, at(1))
        gx0, gy0, px, py = stresses(pa, at(0), ux, uy, uxn, uyn)
        for r in range(n):
            ux, uy = uxn, uyn
            if r < n - 1:
                uxn, uyn = read(sa, 0, at(r + 2)), read(sa, 1, at(r + 2))
                gx, gy, qx, qy = stresses(pa, at(r + 1), ux, uy, uxn, uyn)
            else:
                tx, ty = trace(0), trace(1)
                gx = [jnp.where(sub == 7, tx[c], pltpu.roll(gx0[c], 7, 0)) for c in range(CT)]
                gy = [jnp.where(sub == 7, ty[c], pltpu.roll(gy0[c], 7, 0)) for c in range(CT)]
                qx, qy = px, py
            update(sa, pa, at(r + 1), ux, uy, gx, gy, px, py)
            px, py = qx, qy
        uxs = [read(sb, 0, bt(r)) for r in range(n + 1)]
        uys = [read(sb, 1, bt(r)) for r in range(n + 1)]
        tx, ty = trace(2), trace(3)
        gz, hz, px, py = stresses(pb, bt(n - 1), uxs[n - 1], uys[n - 1], uxs[n], uys[n])
        px = [jnp.where(sub == 0, tx[c], pltpu.roll(px[c], 1, 0)) for c in range(CT)]
        py = [jnp.where(sub == 0, ty[c], pltpu.roll(py[c], 1, 0)) for c in range(CT)]
        for r in range(n):
            if r < n - 1:
                gx, gy, qx, qy = stresses(pb, bt(r), uxs[r], uys[r], uxs[r + 1], uys[r + 1])
            else:
                gx, gy, qx, qy = gz, hz, None, None
            update(sb, pb, bt(r), uxs[r], uys[r], gx, gy, px, py)
            px, py = qx, qy
        return carry

    lax.fori_loop(0, STEPS, body, 0)
    for f in range(6):
        for c in range(CT - 1):
            cols = slice(128 * c, 128 * c + 128)
            scale = 1.0 / DT if f in (2, 3) else None
            for first, block in ((0, sa[f, c, H : 2 * H, :]), (H, keep_ref[f, c, H:, :]), (rows - H, sb[f, c, 0:H, :])):
                out_ref[f, first : first + block.shape[0], cols] = block if scale is None else scale * block


def params(bytes_, flops):
    return dict(
        compiler_params=pltpu.CompilerParams(vmem_limit_bytes=24 * 2**20),
        cost_estimate=pl.CostEstimate(flops=flops, bytes_accessed=bytes_, transcendentals=0),
    )


def ring(count, step):
    return [(i, (i + step) % count) for i in range(count)]


def shards(state, grade, table):
    fields, rows, cols = state.shape
    nx = lax.axis_size("gx")
    ny = lax.axis_size("gy")
    gy = jnp.full((1,), lax.axis_index("gy"), jnp.int32)
    packed = jax.ShapeDtypeStruct((7, rows // PACK, 128), F32)
    to_left, to_right = pl.pallas_call(
        pack_y_kernel,
        out_shape=(packed, packed),
        in_specs=[VMEM, VMEM],
        out_specs=(VMEM, VMEM),
        **params(10**6, 10**5),
    )(state, grade)
    from_left = lax.ppermute(to_right, "gy", ring(ny, 1))
    from_right = lax.ppermute(to_left, "gy", ring(ny, -1))
    strip = jax.ShapeDtypeStruct((7, CT, H, 128), F32)
    edge, to_up, to_down = pl.pallas_call(
        functools.partial(pack_x_kernel, ny),
        out_shape=(jax.ShapeDtypeStruct((7, rows, 128), F32), strip, strip),
        in_specs=[SMEM] + [VMEM] * 4,
        out_specs=(VMEM,) * 3,
        **params(2 * 10**6, 10**5),
    )(gy, state, grade, from_left, from_right)
    top = lax.ppermute(to_down, "gx", ring(nx, 1))
    bottom = lax.ppermute(to_up, "gx", ring(nx, -1))
    keep, tail, trace = pl.pallas_call(
        functools.partial(interior_kernel, ny),
        out_shape=(
            jax.ShapeDtypeStruct((6, CT, rows - H, 128), F32),
            jax.ShapeDtypeStruct((6, CT, H, 128), F32),
            jax.ShapeDtypeStruct((4, CT, H, 128), F32),
        ),
        in_specs=[SMEM] + [VMEM] * 4,
        out_specs=(VMEM,) * 3,
        scratch_shapes=[
            pltpu.VMEM((6, CT, rows + 8, 128), F32),
            pltpu.VMEM((8, CT, rows + 8, 128), F32),
            pltpu.VMEM((2, CT, rows + 8, 128), F32),
            pltpu.VMEM((8, 128), F32),
        ],
        **params(4 * 10**6, 10**9),
    )(gy, table, state, grade, edge)
    return pl.pallas_call(
        functools.partial(exterior_kernel, ny),
        out_shape=jax.ShapeDtypeStruct((fields, rows, cols), F32),
        in_specs=[SMEM] + [VMEM] * 8,
        out_specs=VMEM,
        scratch_shapes=[
            pltpu.VMEM((6, CT, 2 * H + 8, 128), F32),
            pltpu.VMEM((8, CT, 2 * H + 8, 128), F32),
            pltpu.VMEM((6, CT, 2 * H + 8, 128), F32),
            pltpu.VMEM((8, CT, 2 * H + 8, 128), F32),
            pltpu.VMEM((8, 128), F32),
        ],
        **params(4 * 10**6, 10**9),
    )(gy, table, grade, edge, keep, tail, trace, top, bottom)


def solution(mesh):
    placed = (P(None, "gx", "gy"), P("gx", "gy"), P())
    return jax.shard_map(
        shards, mesh=mesh, in_specs=placed, out_specs=P(None, "gx", "gy"), check_vma=False
    )
```

time: 695 us -> 36.3 us (0.05)
  the two profiles are of different devices: /device:TPU:8 before, /device:TPU:14 now
where the time goes in v1:
time: 36.3 us; the launch traced here: 36.2 us
  Pallas kernels  20.2 us (56%)
  starting transfers between devices  7.61 us (21%)
  waiting for transfers between devices  6.29 us (17%)
  local copies, waits for them, and re-layouts  2.05 us (6%)
    pallas_call x1, Pallas kernels, shards(): pl.pallas_call(functools.partial(exterior_kernel, ny), out_shape=jax.Shap...  9.99 us
    pallas_call x1, Pallas kernels, shards(): pl.pallas_call(functools.partial(interior_kernel, ny), out_shape=(jax.Sha...  9.82 us
    ppermute x1, starting transfers between devices, shards(): bottom = lax.ppermute(to_up, 'gx', ring(nx, -1))  5.35 us
    ppermute x1, waiting for transfers between devices, shards(): from_right = lax.ppermute(to_left, 'gy', ring(ny, -1))  4.21 us
    ppermute x1, starting transfers between devices, shards(): from_left = lax.ppermute(to_right, 'gy', ring(ny, 1))  2.18 us
    ppermute x1, waiting for transfers between devices, shards(): from_left = lax.ppermute(to_right, 'gy', ring(ny, 1))  2.07 us
    unnamed x10, local copies, waits for them, and re-layouts  2.05 us
  transfers between devices with their start and end apart: 4, of which 2 were waited for; matrix products, arithmetic and copies ran while one was open for 0% of the time, Pallas kernels for 27%

profile of v1, /device:TPU:14, one launch (start us, length us, event | category | flops | bytes accessed | tf_op | source)
XLA Modules:
  0.0 36.2 jit_solution(10484992507034037723)
XLA Ops:
  0.0 0.0 copy-start
  0.0 1.1 %copy-done = f32[6,64,512]{2,1,0:T(8,128)S(1)} copy-done((f32[6,64,512]{2,1,0:T(8,128)S(1)}, f32[6,64,512]{2,1,0:T(8,128)}, u32[]{:S(2)}) %copy-start) | copy-done | bytes 786456
  1.1 0.0 copy-start.2
  1.1 0.9 %copy-done.2 = s32[64,512]{1,0:T(8,128)S(1)} copy-done((s32[64,512]{1,0:T(8,128)S(1)}, s32[64,512]{1,0:T(8,128)}, u32[]{:S(2)}) %copy-start.2) | copy-done | bytes 131096
  2.0 0.0 copy-start.1
  2.0 0.0 copy-start.3
  2.0 0.2 shard_map.37
  2.2 2.2 %collective-permute-start = (f32[7,16,128]{2,1,0:T(8,128)S(1)}, f32[7,16,128]{2,1,0:T(8,128)S(1)}, u32[]{:S(2)}, u32[]{:S(2)}) collective-permute-start(f32[7,16,128]{2,1,0:T(8,128)S(1)} %get-tuple-element.13), channel_id=1, source_target_pairs={{0,1},{1,2},{2,3},{3,4},{4,5},{5,6},{6,7},{7,0},{8,9},{9,10},{10,1... | collective-permute-start | bytes 172040 | tf_op jit(solution)/shard_map/ppermute | solution.py:388
  4.4 0.0 collective-permute-start.1
  4.4 2.1 %collective-permute-done.from_left_ref = f32[7,16,128]{2,1,0:T(8,128)S(1)} collective-permute-done((f32[7,16,128]{2,1,0:T(8,128)S(1)}, f32[7,16,128]{2,1,0:T(8,128)S(1)}, u32[]{:S(2)}, u32[]{:S(2)}) %collective-permute-start) | collective-permute-done | bytes 57376 | tf_op jit(solution)/shard_map/ppermute | solution.py:388
  6.5 4.2 %collective-permute-done.1.from_right_ref = f32[7,16,128]{2,1,0:T(8,128)S(1)} collective-permute-done((f32[7,16,128]{2,1,0:T(8,128)S(1)}, f32[7,16,128]{2,1,0:T(8,128)S(1)}, u32[]{:S(2)}, u32[]{:S(2)}) %collective-permute-start.1) | collective-permute-done | bytes 57376 | tf_op jit(solution)/shard_map/ppermute | solution.py:389
  10.7 0.0 copy-done.1
  10.7 0.0 copy-done.3
  10.7 0.2 shard_map.38
  10.9 0.0 copy-start.4
  10.9 0.1 collective-permute-start.2
  11.0 5.3 %collective-permute-start.3 = (f32[7,5,24,128]{3,2,1,0:T(8,128)S(1)}, f32[7,5,24,128]{3,2,1,0:T(8,128)S(1)}, u32[]{:S(2)}, u32[]{:S(2)}) collective-permute-start(f32[7,5,24,128]{3,2,1,0:T(8,128)S(1)} %get-tuple-element.20), channel_id=1, source_target_pairs={{0,248},{8,0},{16,8},{24,16},{32,24},{40,32},{48,40},{56,48},{64,5... | collective-permute-start | bytes 1290248 | tf_op jit(solution)/shard_map/ppermute | solution.py:399
  16.3 0.0 copy-done.4
  16.3 9.8 %shard_map.39 = (f32[6,5,40,128]{3,2,1,0:T(8,128)S(1)}, f32[6,5,24,128]{3,2,1,0:T(8,128)S(1)}, f32[4,5,24,128]{3,2,1,0:T(8,128)S(1)}) custom-call(s32[1]{0:T(128)} %bitcast.gy_ref, f32[6,16]{1,0:T(8,128)S(1)} %copy-done.4, f32[6,64,512]{2,1,0:T(8,128)S(1)} %copy-done.1, s32[64,512]{1,0:T(8,128)S(1)} %copy-done.3, f32[7,64,128]{2,1,0:T(8,128)S(1)} %get-tuple-element.15.edge_ref), custom_call_target="tpu_custom_call" | custom-call | flops 1000000000 | bytes 4000000 | tf_op jit(solution)/shard_map/pallas_call | solution.py:400
  26.2 0.0 collective-permute-done.2.top_ref
  26.2 0.0 collective-permute-done.3.bottom_ref
  26.2 10.0 %shard_map.40 = f32[6,64,512]{2,1,0:T(8,128)} custom-call(s32[1]{0:T(128)} %bitcast.gy_ref, f32[6,16]{1,0:T(8,128)S(1)} %copy-done.4, s32[64,512]{1,0:T(8,128)S(1)} %copy-done.3, f32[7,64,128]{2,1,0:T(8,128)S(1)} %get-tuple-element.15.edge_ref, f32[6,5,40,128]{3,2,1,0:T(8,128)S(1)} %get-tuple-element.16.keep_ref, ...), custom_call_target="tpu_custom_call" | custom-call | flops 1000000000 | bytes 4000000 | tf_op jit(solution)/shard_map/pallas_call | solution.py:417
Async XLA Ops:
  0.0 1.1 %copy-start = (f32[6,64,512]{2,1,0:T(8,128)S(1)}, f32[6,64,512]{2,1,0:T(8,128)}, u32[]{:S(2)}) copy-start(f32[6,64,512]{2,1,0:T(8,128)} %state_ref.5) | copy-start | bytes 2359300
  1.1 0.9 %copy-start.2 = (s32[64,512]{1,0:T(8,128)S(1)}, s32[64,512]{1,0:T(8,128)}, u32[]{:S(2)}) copy-start(s32[64,512]{1,0:T(8,128)} %grade_ref.7) | copy-start | bytes 393220
  2.0 8.6 %copy-start.1 = (f32[6,64,512]{2,1,0:T(8,128)S(1)}, f32[6,64,512]{2,1,0:T(8,128)}, u32[]{:S(2)}) copy-start(f32[6,64,512]{2,1,0:T(8,128)} %state_ref.5) | copy-start | bytes 2359300
  2.0 8.6 %copy-start.3 = (s32[64,512]{1,0:T(8,128)S(1)}, s32[64,512]{1,0:T(8,128)}, u32[]{:S(2)}) copy-start(s32[64,512]{1,0:T(8,128)} %grade_ref.7) | copy-start | bytes 393220
  2.2 4.3 %collective-permute-start = (f32[7,16,128]{2,1,0:T(8,128)S(1)}, f32[7,16,128]{2,1,0:T(8,128)S(1)}, u32[]{:S(2)}, u32[]{:S(2)}) collective-permute-start(f32[7,16,128]{2,1,0:T(8,128)S(1)} %get-tuple-element.13), channel_id=1, source_target_pairs={{0,1},{1,2},{2,3},{3,4},{4,5},{5,6},{6,7},{7,0},{8,9},{9,10},{10,1... | collective-permute-start | bytes 172040 | tf_op jit(solution)/shard_map/ppermute | solution.py:388
  4.4 6.3 %collective-permute-start.1 = (f32[7,16,128]{2,1,0:T(8,128)S(1)}, f32[7,16,128]{2,1,0:T(8,128)S(1)}, u32[]{:S(2)}, u32[]{:S(2)}) collective-permute-start(f32[7,16,128]{2,1,0:T(8,128)S(1)} %get-tuple-element.14), channel_id=1, source_target_pairs={{0,7},{1,0},{2,1},{3,2},{4,3},{5,4},{6,5},{7,6},{8,15},{9,8},{10,9... | collective-permute-start | bytes 172040 | tf_op jit(solution)/shard_map/ppermute | solution.py:389
  10.9 5.5 %copy-start.4 = (f32[6,16]{1,0:T(8,128)S(1)}, f32[6,16]{1,0:T(8,128)}, u32[]{:S(2)}) copy-start(f32[6,16]{1,0:T(8,128)} %table_ref.3) | copy-start | bytes 1156
  10.9 15.3 %collective-permute-start.2 = (f32[7,5,24,128]{3,2,1,0:T(8,128)S(1)}, f32[7,5,24,128]{3,2,1,0:T(8,128)S(1)}, u32[]{:S(2)}, u32[]{:S(2)}) collective-permute-start(f32[7,5,24,128]{3,2,1,0:T(8,128)S(1)} %get-tuple-element.19), channel_id=1, source_target_pairs={{0,8},{8,16},{16,24},{24,32},{32,40},{40,48},{48,56},{56,64},{64,7... | collective-permute-start | bytes 1290248 | tf_op jit(solution)/shard_map/ppermute | solution.py:398
  11.0 15.2 %collective-permute-start.3 = (f32[7,5,24,128]{3,2,1,0:T(8,128)S(1)}, f32[7,5,24,128]{3,2,1,0:T(8,128)S(1)}, u32[]{:S(2)}, u32[]{:S(2)}) collective-permute-start(f32[7,5,24,128]{3,2,1,0:T(8,128)S(1)} %get-tuple-element.20), channel_id=1, source_target_pairs={{0,248},{8,0},{16,8},{24,16},{32,24},{40,32},{48,40},{56,48},{64,5... | collective-permute-start | bytes 1290248 | tf_op jit(solution)/shard_map/ppermute | solution.py:399

commit v2 on v1

v2 whole, which is shorter than its diff:
```python
import functools

import jax
import jax.numpy as jnp
from jax import lax
from jax.experimental import pallas as pl
from jax.experimental.pallas import tpu as pltpu
from jax.sharding import PartitionSpec as P

STEPS = 24
DT = 0.2
F32 = jnp.float32
H = 24
CT = 5
EDGE = 4
MAIN = (0, 1, 2, 3)
ALL = (0, 1, 2, 3, 4)
SWAP = 8
MID = 20
PACK = 4

VMEM = pl.BlockSpec(memory_space=pltpu.VMEM)
SMEM = pl.BlockSpec(memory_space=pltpu.SMEM)
ANY = pl.BlockSpec(memory_space=pl.ANY)
HBM = pl.BlockSpec(memory_space=pltpu.HBM)


def lanes():
    return lax.broadcasted_iota(jnp.int32, (8, 128), 1)


def sublanes():
    return lax.broadcasted_iota(jnp.int32, (8, 128), 0)


def edge_live(gy, count):
    right = jnp.where(gy < count - 1, 1, 0)
    left = jnp.where(gy > 0, 1, 0)
    lane = lanes()
    return jnp.where(lane < H, left, jnp.where(lane >= 128 - H, right, 1)) > 0


def pack_y_kernel(state_hbm, grade_hbm, left_ref, right_ref, grade_ref, ends, sems):
    rows, cols = state_hbm.shape[1:]
    group = rows // PACK
    lane = lanes()
    copies = []
    for f in range(6):
        for side, first in enumerate((0, cols - 128)):
            source = state_hbm.at[f, :, pl.ds(first, 128)]
            copies.append(pltpu.make_async_copy(source, ends.at[f, side], sems.at[2 * f + side]))
    copies.append(pltpu.make_async_copy(grade_hbm, grade_ref, sems.at[12]))
    for copy in copies:
        copy.start()

    def read(field, row, side):
        if field < 6:
            return ends[field, side, row : row + 8, :]
        first = side * (cols - 128)
        return grade_ref[row : row + 8, first : first + 128].astype(F32)

    for field in range(7):
        for copy in copies[2 * field : 2 * field + 2]:
            copy.wait()
        for k in range(group // 8):
            to_left = None
            to_right = None
            for q in range(PACK):
                row = q * group + 8 * k
                a = read(field, row, 0)
                b = read(field, row, 1)
                if q:
                    a = pltpu.roll(a, 32 * q, 1)
                b = pltpu.roll(b, 32 * q + H, 1)
                here = lane >= 32 * q
                to_left = a if q == 0 else jnp.where(here, a, to_left)
                to_right = b if q == 0 else jnp.where(here, b, to_right)
            left_ref[field, 8 * k : 8 * k + 8, :] = to_left
            right_ref[field, 8 * k : 8 * k + 8, :] = to_right


def pack_x_kernel(count, gy_ref, state_ref, grade_ref, from_left_ref, from_right_ref, _, edge_ref, up_ref, down_ref):
    rows, cols = state_ref.shape[1:]
    group = rows // PACK
    lane = lanes()
    live = edge_live(gy_ref[0], count)
    for field in range(7):
        for k in range(group // 8):
            right = from_right_ref[field, 8 * k : 8 * k + 8, :]
            left = from_left_ref[field, 8 * k : 8 * k + 8, :]
            for q in range(PACK):
                r = pltpu.roll(right, (128 - H - 32 * q) % 128, 1)
                s = left if q == 0 else pltpu.roll(left, 128 - 32 * q, 1)
                halo = jnp.where(lane < 64, s, r)
                if field < 6:
                    halo = jnp.where(live, halo, 0.0)
                row = q * group + 8 * k
                if field < 6:
                    first = state_ref[field, row : row + 8, 0:128]
                    last = state_ref[field, row : row + 8, cols - 128 : cols]
                else:
                    first = grade_ref[row : row + 8, 0:128].astype(F32)
                    last = grade_ref[row : row + 8, cols - 128 : cols].astype(F32)
                own = jnp.where(lane < 64, pltpu.roll(first, H, 1), pltpu.roll(last, 128 - H, 1))
                both = jnp.where((lane < H) | (lane >= 128 - H), halo, own)
                edge_ref[field, row : row + 8, :] = both
                if row < H:
                    up_ref[field, EDGE, row : row + 8, :] = both
                if row >= rows - H:
                    down_ref[field, EDGE, row - rows + H : row - rows + H + 8, :] = both
    for field in range(7):
        for c in MAIN:
            part = slice(128 * c, 128 * c + 128)
            if field < 6:
                up_ref[field, c] = state_ref[field, 0:H, part]
                down_ref[field, c] = state_ref[field, rows - H : rows, part]
            else:
                up_ref[field, c] = grade_ref[0:H, part].astype(F32)
                down_ref[field, c] = grade_ref[rows - H : rows, part].astype(F32)


def tables(table_ref, tab):
    tab[0:6, 0:16] = table_ref[...]

    def row(q):
        return jnp.broadcast_to(tab[q : q + 1, :], (8, 128))

    rate = row(4)
    return (
        0.25 * row(0),
        0.25 * row(1),
        0.25 * row(2),
        (DT * DT) * row(3),
        1.0 - rate,
        rate * row(5),
    )


def put_raw(pr, tabs, live, grade_of, cols, tiles, first_row, planes_=(0, 1, 3, 5, 6, 7)):
    for k in range(tiles):
        for c in cols:
            grade = grade_of(c, k)
            for t, q in enumerate((0, 1, 3, 5, 6, 7)):
                if q not in planes_:
                    continue
                value = jnp.take_along_axis(tabs[t], grade, axis=1)
                if c == EDGE and q in (5, 7):
                    value = jnp.where(live, value, 0.0)
                pr[q][c][pl.ds(first_row + 8 * k, 8), :] = value


def put_means(pr, live, cols, first_tile, tiles):
    for k in range(first_tile, first_tile + tiles):
        here = pl.ds(8 * k, 8)
        for q in (0, 1, 3):
            sums = {c: pr[q][c][here, :] + pr[q][c][pl.ds(8 * k + 1, 8), :] for c in cols}
            moved = following(sums)
            for c in cols:
                mean = sums[c] + moved[c]
                if c == EDGE:
                    mean = jnp.where(live, mean, 0.0)
                if q == 0:
                    pr[0][c][here, :] = mean
                elif q == 1:
                    pr[1][c][here, :] = 2.0 * mean
                    pr[2][c][here, :] = mean
                else:
                    pr[3][c][here, :] = mean
                    pr[4][c][here, :] = 0.125 * mean


def following(tiles):
    last = lanes() == 127
    rolled = {c: pltpu.roll(x, 127, 1) for c, x in tiles.items()}
    return {c: jnp.where(last, rolled[c + 1], rolled[c]) if c + 1 in MAIN and c in MAIN else rolled[c] for c in tiles}


def preceding(tiles):
    first = lanes() == 0
    rolled = {c: pltpu.roll(x, 1, 1) for c, x in tiles.items()}
    return {c: jnp.where(first, rolled[c - 1], rolled[c]) if c - 1 in MAIN and c in MAIN else rolled[c] for c in tiles}


def read(refs, rows):
    return {c: ref[rows, :] for c, ref in refs.items()}


def stresses(pr, rows, ux, uy, uxn, uyn):
    uxr = following(ux)
    uyr = following(uy)
    lam, mu2, mu, beta, beta8 = [read({c: pr[q][c] for c in ux}, rows) for q in range(5)]
    sxx, sxy, syy = {}, {}, {}
    for c in ux:
        exx = uxn[c] - ux[c]
        eyy = uyr[c] - uy[c]
        g = (uxr[c] - ux[c]) + (uyn[c] - uy[c])
        trace = lam[c] * (exx + eyy)
        sxx[c] = trace + exx * (mu2[c] + beta[c] * (exx * exx))
        syy[c] = trace + eyy * (mu2[c] + beta[c] * (eyy * eyy))
        sxy[c] = g * (mu[c] + beta8[c] * (g * g))
    sxy_l = preceding(sxy)
    syy_l = preceding(syy)
    gx = {c: sxx[c] + (sxy[c] - sxy_l[c]) for c in ux}
    gy = {c: sxy[c] + (syy[c] - syy_l[c]) for c in ux}
    return gx, gy, sxx, sxy


def update(st, pr, rows, ux, uy, gx, gy, px, py):
    dr, om, re = [read({c: pr[q][c] for c in ux}, rows) for q in (5, 6, 7)]
    vx, vy, wx, wy = [read({c: st[q][c] for c in ux}, rows) for q in (2, 3, 4, 5)]
    for c in ux:
        fx = gx[c] - px[c]
        fy = gy[c] - py[c]
        new_vx = vx[c] + dr[c] * (fx - wx[c])
        new_vy = vy[c] + dr[c] * (fy - wy[c])
        st[2][c][rows, :] = new_vx
        st[3][c][rows, :] = new_vy
        st[4][c][rows, :] = om[c] * wx[c] + re[c] * fx
        st[5][c][rows, :] = om[c] * wy[c] + re[c] * fy
        st[0][c][rows, :] = ux[c] + new_vx
        st[1][c][rows, :] = uy[c] + new_vy


def tiles_of(ref, cols):
    return [{c: ref.at[q, c] for c in cols} for q in range(ref.shape[0])]


def swap(st, first_row, rows):
    lane = lanes()
    inner = (lane >= H + MID) & (lane < 128 - H - MID)
    tiles = [pl.ds(8 * k, 8) for k in range(first_row // 8, (first_row + rows) // 8)]
    for f in range(6):
        old = [(st[f][EDGE][here, :], st[f][0][here, :], st[f][MAIN[-1]][here, :]) for here in tiles]
        new = []
        for edge, first, last in old:
            own = jnp.where(lane < 64, pltpu.roll(first, H, 1), pltpu.roll(last, 128 - H, 1))
            new.append((
                jnp.where(inner, own, edge),
                jnp.where(lane < MID, pltpu.roll(edge, 128 - H, 1), first),
                jnp.where(lane >= 128 - MID, pltpu.roll(edge, H, 1), last),
            ))
        for here, (edge, first, last) in zip(tiles, new):
            st[f][EDGE][here, :] = edge
            st[f][0][here, :] = first
            st[f][MAIN[-1]][here, :] = last


def trapezoid(st, pr, ss, cols, rows, groups, trace_ref, tail_ref):
    for g in groups:
        n = rows // 8 - g
        n = n + 1 if n == 8 else n

        def body(k, carry, n=n, g=g):
            base = 4 * g + k

            def at(offset):
                return pl.ds(base + offset, 8, stride=n)

            def u(f, offset):
                return read({c: st[f][c] for c in cols}, at(offset))

            ux, uy, uxn, uyn = u(0, 0), u(1, 0), u(0, 1), u(1, 1)
            gx0, gy0, px, py = stresses(pr, at(0), ux, uy, uxn, uyn)
            for c in cols:
                trace_ref[0, c, pl.ds(base, 1), :] = gx0[c][0:1]
                trace_ref[1, c, pl.ds(base, 1), :] = gy0[c][0:1]
            for r in range(n):
                ux, uy = uxn, uyn
                for c in cols:
                    ss[0, c, at(r), :] = px[c]
                    ss[1, c, at(r), :] = py[c]
                if r < n - 1:
                    uxn, uyn = u(0, r + 2), u(1, r + 2)
                    gx, gy, qx, qy = stresses(pr, at(r + 1), ux, uy, uxn, uyn)
                else:
                    gx = {c: pltpu.roll(v, 7, 0) for c, v in gx0.items()}
                    gy = {c: pltpu.roll(v, 7, 0) for c, v in gy0.items()}
                    qx, qy = px, py
                update(st, pr, at(r + 1), ux, uy, gx, gy, px, py)
                px, py = qx, qy
            row = pl.ds(rows - 2 - base, 1)
            for c in cols:
                for q in range(2):
                    trace_ref[2 + q, c, pl.ds(base, 1), :] = ss[q, c, row, :]
                for f in range(6):
                    tail_ref[f, c, pl.ds(H - 1 - base, 1), :] = st[f][c][row, :]
            return carry

        lax.fori_loop(0, 4, body, 0)


def own_kernel(table_ref, state_ref, grade_ref, st_ref, pr_ref, tail_ref, trace_ref, ss, tab):
    rows = state_ref.shape[1]
    tabs = tables(table_ref, tab)
    st, pr = tiles_of(st_ref, MAIN), tiles_of(pr_ref, MAIN)

    def grade_of(c, k):
        return grade_ref[8 * k : 8 * k + 8, 128 * c : 128 * c + 128]

    put_raw(pr, tabs, None, grade_of, MAIN, rows // 8, 0)
    put_means(pr, None, MAIN, 0, rows // 8)
    for f in range(6):
        for c in MAIN:
            block = state_ref[f, :, 128 * c : 128 * c + 128]
            if f in (2, 3):
                block = DT * block
            st[f][c][0:rows, :] = block
            tail_ref[f, c, H : H + 1, :] = block[rows - 1 : rows]
    trapezoid(st, pr, ss, MAIN, rows, range(SWAP // 4), trace_ref, tail_ref)


def interior_kernel(
    count, gy_ref, table_ref, edge_ref, st_ref, pr_ref, tail_in, trace_in, keep_ref, tail_ref, trace_ref, pe_ref, mid, ss, tab
):
    rows = edge_ref.shape[1]
    live = edge_live(gy_ref[0], count)
    tabs = tables(table_ref, tab)
    st = tiles_of(mid, ALL)
    pr = tiles_of(pr_ref, MAIN)
    for q in range(8):
        pr[q][EDGE] = pe_ref.at[q]

    def grade_of(c, k):
        return edge_ref[6, 8 * k : 8 * k + 8, :].astype(jnp.int32)

    put_raw(pr, tabs, live, grade_of, (EDGE,), rows // 8, 0)
    put_means(pr, live, (EDGE,), 0, rows // 8)
    for f in range(6):
        block = DT * edge_ref[f] if f in (2, 3) else edge_ref[f]
        st[f][EDGE][0:rows, :] = block
        tail_ref[f, EDGE, H : H + 1, :] = block[rows - 1 : rows]
        for c in MAIN:
            st[f][c][0:rows, :] = st_ref[f, c, 0:rows, :]
            tail_ref[f, c] = tail_in[f, c]
    for q in range(4):
        for c in MAIN:
            trace_ref[q, c] = trace_in[q, c]
    trapezoid(st, pr, ss, (EDGE,), rows, range(SWAP // 4), trace_ref, tail_ref)
    swap(st, 0, rows)
    trapezoid(st, pr, ss, ALL, rows, range(SWAP // 4, STEPS // 4), trace_ref, tail_ref)
    for f in range(6):
        for c in ALL:
            keep_ref[f, c] = st[f][c][0 : rows - H, :]


def exterior_kernel(
    count, gy_ref, table_ref, grade_ref, edge_ref, keep_ref, tail_ref, trace_ref, pr_ref, pe_ref, top_ref, bottom_ref,
    out_ref, sa_ref, pa_ref, sb_ref, pb_ref, tab,
):
    rows = grade_ref.shape[0]
    live = edge_live(gy_ref[0], count)
    tabs = tables(table_ref, tab)
    near = H // 8
    sa, pa, sb, pb = [tiles_of(ref, ALL) for ref in (sa_ref, pa_ref, sb_ref, pb_ref)]

    def halo(ref):
        return lambda c, k: ref[6, c, 8 * k : 8 * k + 8, :].astype(jnp.int32)

    def own(row):
        def grade_of(c, k):
            if c == EDGE:
                return edge_ref[6, row : row + 8, :].astype(jnp.int32)
            return grade_ref[row : row + 8, 128 * c : 128 * c + 128]

        return grade_of

    def known(q, c, first, count_):
        return pe_ref[q, first : first + count_, :] if c == EDGE else pr_ref[q, c, first : first + count_, :]

    put_raw(pa, tabs, live, halo(top_ref), ALL, near, 0)
    put_raw(pa, tabs, live, own(0), ALL, 1, H, (0, 1, 3))
    put_means(pa, live, ALL, 0, near)
    put_raw(pb, tabs, live, own(rows - 8), ALL, 1, H - 8, (0, 1, 3))
    put_raw(pb, tabs, live, halo(bottom_ref), ALL, near, H)
    put_means(pb, live, ALL, near - 1, near + 1)
    for q in range(8):
        for c in ALL:
            pa[q][c][H : 2 * H, :] = known(q, c, 0, H)
            whole = H if q > 4 else H - 8
            pb[q][c][0:whole, :] = known(q, c, rows - H, whole)
    for f in range(6):
        for c in ALL:
            top = top_ref[f, c]
            bottom = bottom_ref[f, c]
            if f in (2, 3):
                top = DT * top
                bottom = DT * bottom
            sa[f][c][0:H, :] = top
            sa[f][c][H : 2 * H, :] = keep_ref[f, c, 0:H, :]
            sb[f][c][0:H, :] = tail_ref[f, c, 1 : H + 1, :]
            sb[f][c][H : 2 * H, :] = bottom

    sub = sublanes()
    n = near

    def body(base, carry):
        def at(offset):
            return pl.ds(base + offset, 8, stride=n)

        def bt(offset):
            return pl.ds(H - 1 - base + offset, 8, stride=n)

        def trace(q):
            return [jnp.broadcast_to(trace_ref[q, c, pl.ds(base, 1), :], (8, 128)) for c in ALL]

        ux, uy = read(sa[0], at(0)), read(sa[1], at(0))
        uxn, uyn = read(sa[0], at(1)), read(sa[1], at(1))
        gx0, gy0, px, py = stresses(pa, at(0), ux, uy, uxn, uyn)
        for r in range(n):
            ux, uy = uxn, uyn
            if r < n - 1:
                uxn, uyn = read(sa[0], at(r + 2)), read(sa[1], at(r + 2))
                gx, gy, qx, qy = stresses(pa, at(r + 1), ux, uy, uxn, uyn)
            else:
                tx, ty = trace(0), trace(1)
                gx = {c: jnp.where(sub == 7, tx[c], pltpu.roll(gx0[c], 7, 0)) for c in ALL}
                gy = {c: jnp.where(sub == 7, ty[c], pltpu.roll(gy0[c], 7, 0)) for c in ALL}
                qx, qy = px, py
            update(sa, pa, at(r + 1), ux, uy, gx, gy, px, py)
            px, py = qx, qy
        uxs = [read(sb[0], bt(r)) for r in range(n + 1)]
        uys = [read(sb[1], bt(r)) for r in range(n + 1)]
        tx, ty = trace(2), trace(3)
        gz, hz, px, py = stresses(pb, bt(n - 1), uxs[n - 1], uys[n - 1], uxs[n], uys[n])
        px = {c: jnp.where(sub == 0, tx[c], pltpu.roll(px[c], 1, 0)) for c in ALL}
        py = {c: jnp.where(sub == 0, ty[c], pltpu.roll(py[c], 1, 0)) for c in ALL}
        for r in range(n):
            if r < n - 1:
                gx, gy, qx, qy = stresses(pb, bt(r), uxs[r], uys[r], uxs[r + 1], uys[r + 1])
            else:
                gx, gy, qx, qy = gz, hz, None, None
            update(sb, pb, bt(r), uxs[r], uys[r], gx, gy, px, py)
            px, py = qx, qy
        return carry

    lax.fori_loop(0, SWAP, body, 0)
    swap(sa, SWAP, H)
    swap(sb, H - 2 * SWAP, H + SWAP)
    lax.fori_loop(SWAP, STEPS, body, 0)
    lane = lanes()
    for f in range(6):
        for k in range(rows // 8):
            row = 8 * k

            def final(c):
                if row < H:
                    return sa[f][c][H + row : H + row + 8, :]
                if row < rows - H:
                    return keep_ref[f, c, row : row + 8, :]
                return sb[f][c][row - rows + H : row - rows + H + 8, :]

            edge = final(EDGE)
            for c in MAIN:
                value = final(c)
                if c == 0:
                    value = jnp.where(lane < MID, pltpu.roll(edge, 128 - H, 1), value)
                if c == MAIN[-1]:
                    value = jnp.where(lane >= 128 - MID, pltpu.roll(edge, H, 1), value)
                if f in (2, 3):
                    value = (1.0 / DT) * value
                out_ref[f, row : row + 8, 128 * c : 128 * c + 128] = value


def params(bytes_, flops):
    return dict(
        compiler_params=pltpu.CompilerParams(vmem_limit_bytes=24 * 2**20),
        cost_estimate=pl.CostEstimate(flops=flops, bytes_accessed=bytes_, transcendentals=0),
    )


def ring(count, step):
    return [(i, (i + step) % count) for i in range(count)]


def shards(state, grade, table):
    fields, rows, cols = state.shape
    nx = lax.axis_size("gx")
    ny = lax.axis_size("gy")
    gy = jnp.full((1,), lax.axis_index("gy"), jnp.int32)
    packed = jax.ShapeDtypeStruct((7, rows // PACK, 128), F32)
    to_left, to_right, grade = pl.pallas_call(
        pack_y_kernel,
        out_shape=(packed, packed, jax.ShapeDtypeStruct(grade.shape, grade.dtype)),
        in_specs=[HBM, HBM],
        out_specs=(VMEM,) * 3,
        scratch_shapes=[pltpu.VMEM((6, 2, rows, 128), F32), pltpu.SemaphoreType.DMA((13,))],
        **params(10**6, 10**5),
    )(state, grade)
    from_left = lax.ppermute(to_right, "gy", ring(ny, 1))
    from_right = lax.ppermute(to_left, "gy", ring(ny, -1))
    wide = rows + 16
    st, pr, tail, trace = pl.pallas_call(
        own_kernel,
        out_shape=(
            jax.ShapeDtypeStruct((6, CT - 1, wide, 128), F32),
            jax.ShapeDtypeStruct((8, CT - 1, wide, 128), F32),
            jax.ShapeDtypeStruct((6, CT - 1, H + 8, 128), F32),
            jax.ShapeDtypeStruct((4, CT - 1, H, 128), F32),
        ),
        in_specs=[VMEM] * 3,
        out_specs=(VMEM,) * 4,
        scratch_shapes=[pltpu.VMEM((2, CT - 1, wide, 128), F32), pltpu.VMEM((8, 128), F32)],
        **params(10**7, 10**8),
    )(table, state, grade)
    strip = jax.ShapeDtypeStruct((7, CT, H, 128), F32)
    edge, to_up, to_down = pl.pallas_call(
        functools.partial(pack_x_kernel, ny),
        out_shape=(jax.ShapeDtypeStruct((7, rows, 128), F32), strip, strip),
        in_specs=[SMEM] + [VMEM] * 4 + [ANY],
        out_specs=(VMEM,) * 3,
        **params(2 * 10**6, 10**5),
    )(gy, state, grade, from_left, from_right, trace)
    top = lax.ppermute(to_down, "gx", ring(nx, 1))
    bottom = lax.ppermute(to_up, "gx", ring(nx, -1))
    keep, tail, trace, pe = pl.pallas_call(
        functools.partial(interior_kernel, ny),
        out_shape=(
            jax.ShapeDtypeStruct((6, CT, rows - H, 128), F32),
            jax.ShapeDtypeStruct((6, CT, H + 8, 128), F32),
            jax.ShapeDtypeStruct((4, CT, H, 128), F32),
            jax.ShapeDtypeStruct((8, wide, 128), F32),
        ),
        in_specs=[SMEM] + [VMEM] * 6,
        out_specs=(VMEM,) * 4,
        scratch_shapes=[
            pltpu.VMEM((6, CT, wide, 128), F32),
            pltpu.VMEM((2, CT, wide, 128), F32),
            pltpu.VMEM((8, 128), F32),
        ],
        **params(10**7, 10**8),
    )(gy, table, edge, st, pr, tail, trace)
    reach = 2 * H + 8
    return pl.pallas_call(
        functools.partial(exterior_kernel, ny),
        out_shape=jax.ShapeDtypeStruct((fields, rows, cols), F32),
        in_specs=[SMEM] + [VMEM] * 10,
        out_specs=VMEM,
        scratch_shapes=[pltpu.VMEM((planes, CT, reach, 128), F32) for planes in (6, 8, 6, 8)]
        + [pltpu.VMEM((8, 128), F32)],
        **params(10**7, 10**8),
    )(gy, table, grade, edge, keep, tail, trace, pr, pe, top, bottom)


def solution(mesh):
    placed = (P(None, "gx", "gy"), P("gx", "gy"), P())
    return jax.shard_map(
        shards, mesh=mesh, in_specs=placed, out_specs=P(None, "gx", "gy"), check_vma=False
    )
```

time: 36.3 us -> 34.5 us (0.950); the launches traced: 36.2 us -> 33.8 us
  waiting for transfers between devices: 6.29 us -> 2.42 us
  Pallas kernels: 20.2 us -> 21 us
  local copies, waits for them, and re-layouts: 2.05 us -> 2.73 us
    pallas_call x1 -> x2, Pallas kernels: 0.17 us -> 4.11 us  [the longest x1 3.16 us: shards(): pl.pallas_call(own_kernel, out_shape=(jax.ShapeDtypeStruct((6, CT - 1, wi...]
    pallas_call x1, Pallas kernels: 9.82 us -> 6.31 us  [shards(): pl.pallas_call(functools.partial(interior_kernel, ny), out_shape=(jax.Sha...]
    ppermute x1, waiting for transfers between devices: 2.07 us -> 0.01 us  [shards(): from_left = lax.ppermute(to_right, 'gy', ring(ny, 1))]
    ppermute x1, waiting for transfers between devices: 4.21 us -> 2.41 us  [shards(): from_right = lax.ppermute(to_left, 'gy', ring(ny, -1))]
    unnamed x10 -> x8, local copies, waits for them, and re-layouts: 2.05 us -> 2.73 us
  transfers between devices with their start and end apart: 4 -> 4, of which waited for: 2 -> 1; matrix products, arithmetic and copies ran while one was open for 0% -> 0% of each run, Pallas kernels for 27% -> 28%
where the time goes in v2:
time: 34.5 us; the launch traced here: 33.8 us
  Pallas kernels  21 us (61%)
  starting transfers between devices  7.61 us (22%)
  local copies, waits for them, and re-layouts  2.73 us (8%)
  waiting for transfers between devices  2.42 us (7%)
    pallas_call x1, Pallas kernels, shards(): pl.pallas_call(functools.partial(exterior_kernel, ny), out_shape=jax.Shap...  10.3 us
    pallas_call x1, Pallas kernels, shards(): pl.pallas_call(functools.partial(interior_kernel, ny), out_shape=(jax.Sha...  6.31 us
    ppermute x1, starting transfers between devices, shards(): bottom = lax.ppermute(to_up, 'gx', ring(nx, -1))  5.35 us
    pallas_call x1, Pallas kernels, shards(): pl.pallas_call(own_kernel, out_shape=(jax.ShapeDtypeStruct((6, CT - 1, wi...  3.16 us
    unnamed x8, local copies, waits for them, and re-layouts  2.73 us
    ppermute x1, waiting for transfers between devices, shards(): from_right = lax.ppermute(to_left, 'gy', ring(ny, -1))  2.41 us
    ppermute x1, starting transfers between devices, shards(): from_left = lax.ppermute(to_right, 'gy', ring(ny, 1))  2.18 us
    pallas_call x1, Pallas kernels, shards(): pl.pallas_call(pack_y_kernel, out_shape=(packed, packed, jax.ShapeDtypeSt...  0.95 us
  transfers between devices with their start and end apart: 4, of which 1 were waited for; matrix products, arithmetic and copies ran while one was open for 0% of the time, Pallas kernels for 28%

profile of v2, /device:TPU:14, one launch (start us, length us, event | category | flops | bytes accessed | tf_op | source)
XLA Modules:
  0.0 33.8 jit_solution(11001995988182037009)
XLA Ops:
  0.0 0.0 copy-start
  0.0 1.1 %copy-done = f32[6,64,512]{2,1,0:T(8,128)S(1)} copy-done((f32[6,64,512]{2,1,0:T(8,128)S(1)}, f32[6,64,512]{2,1,0:T(8,128)}, u32[]{:S(2)}) %copy-start) | copy-done | bytes 786456
  1.1 0.0 copy-start.2
  1.1 0.9 %copy-done.2 = s32[64,512]{1,0:T(8,128)S(1)} copy-done((s32[64,512]{1,0:T(8,128)S(1)}, s32[64,512]{1,0:T(8,128)}, u32[]{:S(2)}) %copy-start.2) | copy-done | bytes 131096
  2.0 0.0 copy-start.1
  2.0 0.9 %shard_map.37 = (f32[7,16,128]{2,1,0:T(8,128)S(1)}, f32[7,16,128]{2,1,0:T(8,128)S(1)}, s32[64,512]{1,0:T(8,128)S(1)}) custom-call(f32[6,64,512]{2,1,0:T(8,128)S(1)} %copy-done, s32[64,512]{1,0:T(8,128)S(1)} %copy-done.2), custom_call_target="tpu_custom_call" | custom-call | flops 100000 | bytes 1000000 | tf_op jit(solution)/shard_map/pallas_call | solution.py:481
  3.0 2.2 %collective-permute-start = (f32[7,16,128]{2,1,0:T(8,128)S(1)}, f32[7,16,128]{2,1,0:T(8,128)S(1)}, u32[]{:S(2)}, u32[]{:S(2)}) collective-permute-start(f32[7,16,128]{2,1,0:T(8,128)S(1)} %get-tuple-element.20), channel_id=1, source_target_pairs={{0,1},{1,2},{2,3},{3,4},{4,5},{5,6},{6,7},{7,0},{8,9},{9,10},{10,1... | collective-permute-start | bytes 172040 | tf_op jit(solution)/shard_map/ppermute | solution.py:489
  5.2 0.0 collective-permute-start.1
  5.2 0.0 copy-done.1
  5.2 0.0 copy-start.3
  5.2 0.7 %copy-done.3 = f32[6,16]{1,0:T(8,128)S(1)} copy-done((f32[6,16]{1,0:T(8,128)S(1)}, f32[6,16]{1,0:T(8,128)}, u32[]{:S(2)}) %copy-start.3) | copy-done | bytes 408
  5.9 3.2 %shard_map.38 = (f32[6,4,80,128]{3,2,1,0:T(8,128)S(1)}, f32[8,4,80,128]{3,2,1,0:T(8,128)S(1)}, f32[6,4,32,128]{3,2,1,0:T(8,128)S(1)}, f32[4,4,24,128]{3,2,1,0:T(8,128)S(1)}) custom-call(f32[6,16]{1,0:T(8,128)S(1)} %copy-done.3, f32[6,64,512]{2,1,0:T(8,128)S(1)} %copy-done.1, s32[64,512]{1,0:T(8,128)S(1)} %get-tuple-element.19.grade_ref), custom_call_target="tpu_custom_call" | custom-call | flops 100000000 | bytes 10000000 | tf_op jit(solution)/shard_map/pallas_call | solution.py:492
  9.0 0.0 collective-permute-done.from_left_ref
  9.0 2.4 %collective-permute-done.1.from_right_ref = f32[7,16,128]{2,1,0:T(8,128)S(1)} collective-permute-done((f32[7,16,128]{2,1,0:T(8,128)S(1)}, f32[7,16,128]{2,1,0:T(8,128)S(1)}, u32[]{:S(2)}, u32[]{:S(2)}) %collective-permute-start.1) | collective-permute-done | bytes 57376 | tf_op jit(solution)/shard_map/ppermute | solution.py:490
  11.5 0.3 shard_map.39
  11.8 0.1 collective-permute-start.2
  11.8 5.3 %collective-permute-start.3 = (f32[7,5,24,128]{3,2,1,0:T(8,128)S(1)}, f32[7,5,24,128]{3,2,1,0:T(8,128)S(1)}, u32[]{:S(2)}, u32[]{:S(2)}) collective-permute-start(f32[7,5,24,128]{3,2,1,0:T(8,128)S(1)} %get-tuple-element.32), channel_id=1, source_target_pairs={{0,248},{8,0},{16,8},{24,16},{32,24},{40,32},{48,40},{56,48},{64,5... | collective-permute-start | bytes 1290248 | tf_op jit(solution)/shard_map/ppermute | solution.py:514
  17.2 6.3 %shard_map.40 = (f32[6,5,40,128]{3,2,1,0:T(8,128)S(1)}, f32[6,5,32,128]{3,2,1,0:T(8,128)S(1)}, f32[4,5,24,128]{3,2,1,0:T(8,128)S(1)}, f32[8,80,128]{2,1,0:T(8,128)S(1)}) custom-call(s32[1]{0:T(128)} %bitcast.gy_ref, f32[6,16]{1,0:T(8,128)S(1)} %copy-done.3, f32[7,64,128]{2,1,0:T(8,128)S(1)} %get-tuple-element.23.edge_ref, ...), custom_call_target="tpu_custom_call" | custom-call | flops 100000000 | bytes 10000000 | tf_op jit(solution)/shard_map/pallas_call | solution.py:515
  23.5 0.0 collective-permute-done.2.top_ref
  23.5 0.0 collective-permute-done.3.bottom_ref
  23.5 10.3 %shard_map.41 = f32[6,64,512]{2,1,0:T(8,128)} custom-call(s32[1]{0:T(128)} %bitcast.gy_ref, f32[6,16]{1,0:T(8,128)S(1)} %copy-done.3, s32[64,512]{1,0:T(8,128)S(1)} %get-tuple-element.19.grade_ref, f32[7,64,128]{2,1,0:T(8,128)S(1)} %get-tuple-element.23.edge_ref, f32[6,5,40,128]{3,2,1,0:T(8,128)S(1)} %get-tuple-element.27.keep_ref, ...), custom_call_target="tpu_custom_call" | custom-call | flops 100000000 | bytes 10000000 | tf_op jit(solution)/shard_map/pallas_call | solution.py:533
Async XLA Ops:
  0.0 1.1 %copy-start = (f32[6,64,512]{2,1,0:T(8,128)S(1)}, f32[6,64,512]{2,1,0:T(8,128)}, u32[]{:S(2)}) copy-start(f32[6,64,512]{2,1,0:T(8,128)} %state_ref.3) | copy-start | bytes 2359300
  1.1 0.9 %copy-start.2 = (s32[64,512]{1,0:T(8,128)S(1)}, s32[64,512]{1,0:T(8,128)}, u32[]{:S(2)}) copy-start(s32[64,512]{1,0:T(8,128)} %grade_hbm.1) | copy-start | bytes 393220
  2.0 3.1 %copy-start.1 = (f32[6,64,512]{2,1,0:T(8,128)S(1)}, f32[6,64,512]{2,1,0:T(8,128)}, u32[]{:S(2)}) copy-start(f32[6,64,512]{2,1,0:T(8,128)} %state_ref.3) | copy-start | bytes 2359300
  3.0 6.0 %collective-permute-start = (f32[7,16,128]{2,1,0:T(8,128)S(1)}, f32[7,16,128]{2,1,0:T(8,128)S(1)}, u32[]{:S(2)}, u32[]{:S(2)}) collective-permute-start(f32[7,16,128]{2,1,0:T(8,128)S(1)} %get-tuple-element.20), channel_id=1, source_target_pairs={{0,1},{1,2},{2,3},{3,4},{4,5},{5,6},{6,7},{7,0},{8,9},{9,10},{10,1... | collective-permute-start | bytes 172040 | tf_op jit(solution)/shard_map/ppermute | solution.py:489
  5.2 6.3 %collective-permute-start.1 = (f32[7,16,128]{2,1,0:T(8,128)S(1)}, f32[7,16,128]{2,1,0:T(8,128)S(1)}, u32[]{:S(2)}, u32[]{:S(2)}) collective-permute-start(f32[7,16,128]{2,1,0:T(8,128)S(1)} %get-tuple-element.21), channel_id=1, source_target_pairs={{0,7},{1,0},{2,1},{3,2},{4,3},{5,4},{6,5},{7,6},{8,15},{9,8},{10,9... | collective-permute-start | bytes 172040 | tf_op jit(solution)/shard_map/ppermute | solution.py:490
  5.2 0.7 %copy-start.3 = (f32[6,16]{1,0:T(8,128)S(1)}, f32[6,16]{1,0:T(8,128)}, u32[]{:S(2)}) copy-start(f32[6,16]{1,0:T(8,128)} %table_ref.5) | copy-start | bytes 1156
  11.8 11.8 %collective-permute-start.2 = (f32[7,5,24,128]{3,2,1,0:T(8,128)S(1)}, f32[7,5,24,128]{3,2,1,0:T(8,128)S(1)}, u32[]{:S(2)}, u32[]{:S(2)}) collective-permute-start(f32[7,5,24,128]{3,2,1,0:T(8,128)S(1)} %get-tuple-element.31), channel_id=1, source_target_pairs={{0,8},{8,16},{16,24},{24,32},{32,40},{40,48},{48,56},{56,64},{64,7... | collective-permute-start | bytes 1290248 | tf_op jit(solution)/shard_map/ppermute | solution.py:513
  11.8 11.7 %collective-permute-start.3 = (f32[7,5,24,128]{3,2,1,0:T(8,128)S(1)}, f32[7,5,24,128]{3,2,1,0:T(8,128)S(1)}, u32[]{:S(2)}, u32[]{:S(2)}) collective-permute-start(f32[7,5,24,128]{3,2,1,0:T(8,128)S(1)} %get-tuple-element.32), channel_id=1, source_target_pairs={{0,248},{8,0},{16,8},{24,16},{32,24},{40,32},{48,40},{56,48},{64,5... | collective-permute-start | bytes 1290248 | tf_op jit(solution)/shard_map/ppermute | solution.py:514

commit v3 on v2

--- a/solution.py
+++ b/solution.py
@@ -22,7 +22,6 @@
 VMEM = pl.BlockSpec(memory_space=pltpu.VMEM)
 SMEM = pl.BlockSpec(memory_space=pltpu.SMEM)
 ANY = pl.BlockSpec(memory_space=pl.ANY)
-HBM = pl.BlockSpec(memory_space=pltpu.HBM)
 
 
 def lanes():
@@ -40,7 +39,7 @@
     return jnp.where(lane < H, left, jnp.where(lane >= 128 - H, right, 1)) > 0
 
 
-def pack_y_kernel(state_hbm, grade_hbm, left_ref, right_ref, grade_ref, ends, sems):
+def pack_y_kernel(state_hbm, grade_hbm, table_hbm, left_ref, right_ref, grade_ref, table_ref, ends, sems):
     rows, cols = state_hbm.shape[1:]
     group = rows // PACK
     lane = lanes()
@@ -50,6 +49,7 @@
             source = state_hbm.at[f, :, pl.ds(first, 128)]
             copies.append(pltpu.make_async_copy(source, ends.at[f, side], sems.at[2 * f + side]))
     copies.append(pltpu.make_async_copy(grade_hbm, grade_ref, sems.at[12]))
+    copies.append(pltpu.make_async_copy(table_hbm, table_ref, sems.at[13]))
     for copy in copies:
         copy.start()
 
@@ -345,7 +345,7 @@
 
 def exterior_kernel(
     count, gy_ref, table_ref, grade_ref, edge_ref, keep_ref, tail_ref, trace_ref, pr_ref, pe_ref, top_ref, bottom_ref,
-    out_ref, sa_ref, pa_ref, sb_ref, pb_ref, tab,
+    out_ref, sa_ref, pa_ref, sb_ref, pb_ref, hold, tab,
 ):
     rows = grade_ref.shape[0]
     live = edge_live(gy_ref[0], count)
@@ -393,15 +393,39 @@
     sub = sublanes()
     n = near
 
-    def body(base, carry):
+    def trace(q, base):
+        return [jnp.broadcast_to(trace_ref[q, c, pl.ds(base, 1), :], (8, 128)) for c in ALL]
+
+    def b_rows(base, offset):
+        return pl.ds(jnp.maximum(H - 1 - base, 0) + offset, 8, stride=n)
+
+    def b_stress(base):
+        ux = [read(sb[0], b_rows(base, r)) for r in range(n + 1)]
+        uy = [read(sb[1], b_rows(base, r)) for r in range(n + 1)]
+        for r in range(n):
+            found = stresses(pb, b_rows(base, r), ux[r], uy[r], ux[r + 1], uy[r + 1])
+            for q in range(4):
+                for c in ALL:
+                    hold[q, c, 8 * r : 8 * r + 8, :] = found[q][c]
+
+    def b_update(base):
+        def held(q, r):
+            return {c: hold[q, c, 8 * r : 8 * r + 8, :] for c in ALL}
+
+        for r in range(n):
+            if r:
+                px, py = held(2, r - 1), held(3, r - 1)
+            else:
+                tx, ty = trace(2, base), trace(3, base)
+                lx, ly = held(2, n - 1), held(3, n - 1)
+                px = {c: jnp.where(sub == 0, tx[c], pltpu.roll(lx[c], 1, 0)) for c in ALL}
+                py = {c: jnp.where(sub == 0, ty[c], pltpu.roll(ly[c], 1, 0)) for c in ALL}
+            rows_ = b_rows(base, r)
+            update(sb, pb, rows_, read(sb[0], rows_), read(sb[1], rows_), held(0, r), held(1, r), px, py)
+
+    def a_step(base):
         def at(offset):
             return pl.ds(base + offset, 8, stride=n)
-
-        def bt(offset):
-            return pl.ds(H - 1 - base + offset, 8, stride=n)
-
-        def trace(q):
-            return [jnp.broadcast_to(trace_ref[q, c, pl.ds(base, 1), :], (8, 128)) for c in ALL]
 
         ux, uy = read(sa[0], at(0)), read(sa[1], at(0))
         uxn, uyn = read(sa[0], at(1)), read(sa[1], at(1))
@@ -412,30 +436,24 @@
                 uxn, uyn = read(sa[0], at(r + 2)), read(sa[1], at(r + 2))
                 gx, gy, qx, qy = stresses(pa, at(r + 1), ux, uy, uxn, uyn)
             else:
-                tx, ty = trace(0), trace(1)
+                tx, ty = trace(0, base), trace(1, base)
                 gx = {c: jnp.where(sub == 7, tx[c], pltpu.roll(gx0[c], 7, 0)) for c in ALL}
                 gy = {c: jnp.where(sub == 7, ty[c], pltpu.roll(gy0[c], 7, 0)) for c in ALL}
                 qx, qy = px, py
             update(sa, pa, at(r + 1), ux, uy, gx, gy, px, py)
             px, py = qx, qy
-        uxs = [read(sb[0], bt(r)) for r in range(n + 1)]
-        uys = [read(sb[1], bt(r)) for r in range(n + 1)]
-        tx, ty = trace(2), trace(3)
-        gz, hz, px, py = stresses(pb, bt(n - 1), uxs[n - 1], uys[n - 1], uxs[n], uys[n])
-        px = {c: jnp.where(sub == 0, tx[c], pltpu.roll(px[c], 1, 0)) for c in ALL}
-        py = {c: jnp.where(sub == 0, ty[c], pltpu.roll(py[c], 1, 0)) for c in ALL}
-        for r in range(n):
-            if r < n - 1:
-                gx, gy, qx, qy = stresses(pb, bt(r), uxs[r], uys[r], uxs[r + 1], uys[r + 1])
-            else:
-                gx, gy, qx, qy = gz, hz, None, None
-            update(sb, pb, bt(r), uxs[r], uys[r], gx, gy, px, py)
-            px, py = qx, qy
+
+    def body(base, carry):
+        b_update(base)
+        a_step(base)
+        b_stress(base + 1)
         return carry
 
+    b_stress(0)
     lax.fori_loop(0, SWAP, body, 0)
     swap(sa, SWAP, H)
     swap(sb, H - 2 * SWAP, H + SWAP)
+    b_stress(SWAP)
     lax.fori_loop(SWAP, STEPS, body, 0)
     lane = lanes()
     for f in range(6):
@@ -461,9 +479,9 @@
                 out_ref[f, row : row + 8, 128 * c : 128 * c + 128] = value
 
 
-def params(bytes_, flops):
+def params(bytes_, flops, mib=24):
     return dict(
-        compiler_params=pltpu.CompilerParams(vmem_limit_bytes=24 * 2**20),
+        compiler_params=pltpu.CompilerParams(vmem_limit_bytes=int(mib * 2**20)),
         cost_estimate=pl.CostEstimate(flops=flops, bytes_accessed=bytes_, transcendentals=0),
     )
 
@@ -478,14 +496,19 @@
     ny = lax.axis_size("gy")
     gy = jnp.full((1,), lax.axis_index("gy"), jnp.int32)
     packed = jax.ShapeDtypeStruct((7, rows // PACK, 128), F32)
-    to_left, to_right, grade = pl.pallas_call(
+    to_left, to_right, grade, table = pl.pallas_call(
         pack_y_kernel,
-        out_shape=(packed, packed, jax.ShapeDtypeStruct(grade.shape, grade.dtype)),
-        in_specs=[HBM, HBM],
-        out_specs=(VMEM,) * 3,
-        scratch_shapes=[pltpu.VMEM((6, 2, rows, 128), F32), pltpu.SemaphoreType.DMA((13,))],
-        **params(10**6, 10**5),
-    )(state, grade)
+        out_shape=(
+            packed,
+            packed,
+            jax.ShapeDtypeStruct(grade.shape, grade.dtype),
+            jax.ShapeDtypeStruct(table.shape, table.dtype),
+        ),
+        in_specs=[ANY] * 3,
+        out_specs=(VMEM,) * 4,
+        scratch_shapes=[pltpu.VMEM((6, 2, rows, 128), F32), pltpu.SemaphoreType.DMA((14,))],
+        **params(10**6, 10**5, 53.6),
+    )(state, grade, table)
     from_left = lax.ppermute(to_right, "gy", ring(ny, 1))
     from_right = lax.ppermute(to_left, "gy", ring(ny, -1))
     wide = rows + 16
@@ -536,7 +559,7 @@
         in_specs=[SMEM] + [VMEM] * 10,
         out_specs=VMEM,
         scratch_shapes=[pltpu.VMEM((planes, CT, reach, 128), F32) for planes in (6, 8, 6, 8)]
-        + [pltpu.VMEM((8, 128), F32)],
+        + [pltpu.VMEM((4, CT, H, 128), F32), pltpu.VMEM((8, 128), F32)],
         **params(10**7, 10**8),
     )(gy, table, grade, edge, keep, tail, trace, pr, pe, top, bottom)
 

time: 34.5 us -> 33.1 us (0.959); the launches traced: 33.8 us -> 33 us
  local copies, waits for them, and re-layouts: 2.73 us -> 0.76 us
  waiting for transfers between devices: 2.42 us -> 3.11 us
  Pallas kernels: 21 us -> 21.4 us
    unnamed x8 -> x4, local copies, waits for them, and re-layouts: 2.73 us -> 0.76 us
    ppermute x1, waiting for transfers between devices: 2.41 us -> 3.1 us  [shards(): from_right = lax.ppermute(to_left, 'gy', ring(ny, -1))]
    pallas_call x1, Pallas kernels: 0.95 us -> 1.49 us  [shards(): pl.pallas_call(pack_y_kernel, out_shape=(packed, packed, jax.ShapeDtypeSt...]
  transfers between devices with their start and end apart: 4 -> 4, of which waited for: 1 -> 1; matrix products, arithmetic and copies ran while one was open for 0% -> 0% of each run, Pallas kernels for 28% -> 29%
where the time goes in v3:
time: 33.1 us; the launch traced here: 33 us
  Pallas kernels  21.4 us (65%)
  starting transfers between devices  7.61 us (23%)
  waiting for transfers between devices  3.11 us (9%)
  local copies, waits for them, and re-layouts  0.76 us (2%)
    pallas_call x1, Pallas kernels, shards(): pl.pallas_call(functools.partial(exterior_kernel, ny), out_shape=jax.Shap...  10.2 us
    pallas_call x1, Pallas kernels, shards(): pl.pallas_call(functools.partial(interior_kernel, ny), out_shape=(jax.Sha...  6.31 us
    ppermute x1, starting transfers between devices, shards(): bottom = lax.ppermute(to_up, 'gx', ring(nx, -1))  5.35 us
    pallas_call x1, Pallas kernels, shards(): pl.pallas_call(own_kernel, out_shape=(jax.ShapeDtypeStruct((6, CT - 1, wi...  3.17 us
    ppermute x1, waiting for transfers between devices, shards(): from_right = lax.ppermute(to_left, 'gy', ring(ny, -1))  3.1 us
    ppermute x1, starting transfers between devices, shards(): from_left = lax.ppermute(to_right, 'gy', ring(ny, 1))  2.18 us
    pallas_call x1, Pallas kernels, shards(): pl.pallas_call(pack_y_kernel, out_shape=(packed, packed, jax.ShapeDtypeSt...  1.49 us
    unnamed x4, local copies, waits for them, and re-layouts  0.76 us
  transfers between devices with their start and end apart: 4, of which 1 were waited for; matrix products, arithmetic and copies ran while one was open for 0% of the time, Pallas kernels for 29%

profile of v3, /device:TPU:14, one launch (start us, length us, event | category | flops | bytes accessed | tf_op | source)
XLA Modules:
  0.0 33.0 jit_solution(7880297547163297671)
XLA Ops:
  0.0 0.0 copy-start
  0.0 0.0 copy-start.1
  0.0 0.8 %copy-done.1 = f32[6,16]{1,0:T(8,128)S(1)} copy-done((f32[6,16]{1,0:T(8,128)S(1)}, f32[6,16]{1,0:T(8,128)}, u32[]{:S(2)}) %copy-start.1) | copy-done | bytes 408
  0.8 1.5 %shard_map.37 = (f32[7,16,128]{2,1,0:T(8,128)S(1)}, f32[7,16,128]{2,1,0:T(8,128)S(1)}, s32[64,512]{1,0:T(8,128)S(1)}, f32[6,16]{1,0:T(8,128)S(1)}) custom-call(f32[6,64,512]{2,1,0:T(8,128)} %state_ref.3, s32[64,512]{1,0:T(8,128)} %grade_hbm.1, f32[6,16]{1,0:T(8,128)S(1)} %copy-done.1), custom_call_target="tpu_custom_call" | custom-call | flops 100000 | bytes 1000000 | tf_op jit(solution)/shard_map/pallas_call | solution.py:499
  2.3 2.2 %collective-permute-start = (f32[7,16,128]{2,1,0:T(8,128)S(1)}, f32[7,16,128]{2,1,0:T(8,128)S(1)}, u32[]{:S(2)}, u32[]{:S(2)}) collective-permute-start(f32[7,16,128]{2,1,0:T(8,128)S(1)} %get-tuple-element.22), channel_id=1, source_target_pairs={{0,1},{1,2},{2,3},{3,4},{4,5},{5,6},{6,7},{7,0},{8,9},{9,10},{10,1... | collective-permute-start | bytes 172040 | tf_op jit(solution)/shard_map/ppermute | solution.py:512
  4.4 0.0 collective-permute-start.1
  4.4 0.0 copy-done
  4.4 3.2 %shard_map.38 = (f32[6,4,80,128]{3,2,1,0:T(8,128)S(1)}, f32[8,4,80,128]{3,2,1,0:T(8,128)S(1)}, f32[6,4,32,128]{3,2,1,0:T(8,128)S(1)}, f32[4,4,24,128]{3,2,1,0:T(8,128)S(1)}) custom-call(f32[6,16]{1,0:T(8,128)S(1)} %get-tuple-element.20.table_ref, f32[6,64,512]{2,1,0:T(8,128)S(1)} %copy-done, s32[64,512]{1,0:T(8,128)S(1)} %get-tuple-element.21.grade_ref), custom_call_target="tpu_custom_call" | custom-call | flops 100000000 | bytes 10000000 | tf_op jit(solution)/shard_map/pallas_call | solution.py:515
  7.6 0.0 collective-permute-done.from_left_ref
  7.6 3.1 %collective-permute-done.1.from_right_ref = f32[7,16,128]{2,1,0:T(8,128)S(1)} collective-permute-done((f32[7,16,128]{2,1,0:T(8,128)S(1)}, f32[7,16,128]{2,1,0:T(8,128)S(1)}, u32[]{:S(2)}, u32[]{:S(2)}) %collective-permute-start.1) | collective-permute-done | bytes 57376 | tf_op jit(solution)/shard_map/ppermute | solution.py:513
  10.7 0.3 shard_map.39
  11.0 0.1 collective-permute-start.2
  11.1 5.3 %collective-permute-start.3 = (f32[7,5,24,128]{3,2,1,0:T(8,128)S(1)}, f32[7,5,24,128]{3,2,1,0:T(8,128)S(1)}, u32[]{:S(2)}, u32[]{:S(2)}) collective-permute-start(f32[7,5,24,128]{3,2,1,0:T(8,128)S(1)} %get-tuple-element.34), channel_id=1, source_target_pairs={{0,248},{8,0},{16,8},{24,16},{32,24},{40,32},{48,40},{56,48},{64,5... | collective-permute-start | bytes 1290248 | tf_op jit(solution)/shard_map/ppermute | solution.py:537
  16.5 6.3 %shard_map.40 = (f32[6,5,40,128]{3,2,1,0:T(8,128)S(1)}, f32[6,5,32,128]{3,2,1,0:T(8,128)S(1)}, f32[4,5,24,128]{3,2,1,0:T(8,128)S(1)}, f32[8,80,128]{2,1,0:T(8,128)S(1)}) custom-call(s32[1]{0:T(128)} %bitcast.gy_ref, f32[6,16]{1,0:T(8,128)S(1)} %get-tuple-element.20.table_ref, f32[7,64,128]{2,1,0:T(8,128)S(1)} %get-tuple-element.25.edge_ref, ...), custom_call_target="tpu_custom_call" | custom-call | flops 100000000 | bytes 10000000 | tf_op jit(solution)/shard_map/pallas_call | solution.py:538
  22.8 0.0 collective-permute-done.2.top_ref
  22.8 0.0 collective-permute-done.3.bottom_ref
  22.8 10.2 %shard_map.41 = f32[6,64,512]{2,1,0:T(8,128)} custom-call(s32[1]{0:T(128)} %bitcast.gy_ref, f32[6,16]{1,0:T(8,128)S(1)} %get-tuple-element.20.table_ref, s32[64,512]{1,0:T(8,128)S(1)} %get-tuple-element.21.grade_ref, f32[7,64,128]{2,1,0:T(8,128)S(1)} %get-tuple-element.25.edge_ref, f32[6,5,40,128]{3,2,1,0:T(8,128)S(1)} %get-tuple-element.29.keep_ref, ...), custom_call_target="tpu_custom_call" | custom-call | flops 100000000 | bytes 10000000 | tf_op jit(solution)/shard_map/pallas_call | solution.py:556
Async XLA Ops:
  0.0 4.4 %copy-start = (f32[6,64,512]{2,1,0:T(8,128)S(1)}, f32[6,64,512]{2,1,0:T(8,128)}, u32[]{:S(2)}) copy-start(f32[6,64,512]{2,1,0:T(8,128)} %state_ref.3) | copy-start | bytes 2359300
  0.0 0.8 %copy-start.1 = (f32[6,16]{1,0:T(8,128)S(1)}, f32[6,16]{1,0:T(8,128)}, u32[]{:S(2)}) copy-start(f32[6,16]{1,0:T(8,128)} %table_hbm.1) | copy-start | bytes 1156
  2.3 5.4 %collective-permute-start = (f32[7,16,128]{2,1,0:T(8,128)S(1)}, f32[7,16,128]{2,1,0:T(8,128)S(1)}, u32[]{:S(2)}, u32[]{:S(2)}) collective-permute-start(f32[7,16,128]{2,1,0:T(8,128)S(1)} %get-tuple-element.22), channel_id=1, source_target_pairs={{0,1},{1,2},{2,3},{3,4},{4,5},{5,6},{6,7},{7,0},{8,9},{9,10},{10,1... | collective-permute-start | bytes 172040 | tf_op jit(solution)/shard_map/ppermute | solution.py:512
  4.4 6.3 %collective-permute-start.1 = (f32[7,16,128]{2,1,0:T(8,128)S(1)}, f32[7,16,128]{2,1,0:T(8,128)S(1)}, u32[]{:S(2)}, u32[]{:S(2)}) collective-permute-start(f32[7,16,128]{2,1,0:T(8,128)S(1)} %get-tuple-element.23), channel_id=1, source_target_pairs={{0,7},{1,0},{2,1},{3,2},{4,3},{5,4},{6,5},{7,6},{8,15},{9,8},{10,9... | collective-permute-start | bytes 172040 | tf_op jit(solution)/shard_map/ppermute | solution.py:513
  11.0 11.8 %collective-permute-start.2 = (f32[7,5,24,128]{3,2,1,0:T(8,128)S(1)}, f32[7,5,24,128]{3,2,1,0:T(8,128)S(1)}, u32[]{:S(2)}, u32[]{:S(2)}) collective-permute-start(f32[7,5,24,128]{3,2,1,0:T(8,128)S(1)} %get-tuple-element.33), channel_id=1, source_target_pairs={{0,8},{8,16},{16,24},{24,32},{32,40},{40,48},{48,56},{56,64},{64,7... | collective-permute-start | bytes 1290248 | tf_op jit(solution)/shard_map/ppermute | solution.py:536
  11.1 11.7 %collective-permute-start.3 = (f32[7,5,24,128]{3,2,1,0:T(8,128)S(1)}, f32[7,5,24,128]{3,2,1,0:T(8,128)S(1)}, u32[]{:S(2)}, u32[]{:S(2)}) collective-permute-start(f32[7,5,24,128]{3,2,1,0:T(8,128)S(1)} %get-tuple-element.34), channel_id=1, source_target_pairs={{0,248},{8,0},{16,8},{24,16},{32,24},{40,32},{48,40},{56,48},{64,5... | collective-permute-start | bytes 1290248 | tf_op jit(solution)/shard_map/ppermute | solution.py:537

commit v4 on v3

--- a/solution.py
+++ b/solution.py
@@ -336,7 +336,7 @@
         for c in MAIN:
             trace_ref[q, c] = trace_in[q, c]
     trapezoid(st, pr, ss, (EDGE,), rows, range(SWAP // 4), trace_ref, tail_ref)
-    swap(st, 0, rows)
+    swap(st, SWAP, rows - 2 * SWAP)
     trapezoid(st, pr, ss, ALL, rows, range(SWAP // 4, STEPS // 4), trace_ref, tail_ref)
     for f in range(6):
         for c in ALL:

time: 33.1 us -> 33 us (level)
  no operation moved by 1% of the time
where the time goes in v4:
time: 33 us; the launch traced here: 32.9 us
  Pallas kernels  21.4 us (65%)
  starting transfers between devices  7.61 us (23%)
  waiting for transfers between devices  3.11 us (9%)
  local copies, waits for them, and re-layouts  0.76 us (2%)
    pallas_call x1, Pallas kernels, shards(): pl.pallas_call(functools.partial(exterior_kernel, ny), out_shape=jax.Shap...  10.2 us
    pallas_call x1, Pallas kernels, shards(): pl.pallas_call(functools.partial(interior_kernel, ny), out_shape=(jax.Sha...  6.26 us
    ppermute x1, starting transfers between devices, shards(): bottom = lax.ppermute(to_up, 'gx', ring(nx, -1))  5.35 us
    pallas_call x1, Pallas kernels, shards(): pl.pallas_call(own_kernel, out_shape=(jax.ShapeDtypeStruct((6, CT - 1, wi...  3.17 us
    ppermute x1, waiting for transfers between devices, shards(): from_right = lax.ppermute(to_left, 'gy', ring(ny, -1))  3.1 us
    ppermute x1, starting transfers between devices, shards(): from_left = lax.ppermute(to_right, 'gy', ring(ny, 1))  2.18 us
    pallas_call x1, Pallas kernels, shards(): pl.pallas_call(pack_y_kernel, out_shape=(packed, packed, jax.ShapeDtypeSt...  1.49 us
    unnamed x4, local copies, waits for them, and re-layouts  0.76 us
  transfers between devices with their start and end apart: 4, of which 1 were waited for; matrix products, arithmetic and copies ran while one was open for 0% of the time, Pallas kernels for 29%

profile of v4, /device:TPU:14, one launch (start us, length us, event | category | flops | bytes accessed | tf_op | source)
XLA Modules:
  0.0 32.9 jit_solution(3619888254445953916)
XLA Ops:
  0.0 0.0 copy-start
  0.0 0.0 copy-start.1
  0.0 0.8 %copy-done.1 = f32[6,16]{1,0:T(8,128)S(1)} copy-done((f32[6,16]{1,0:T(8,128)S(1)}, f32[6,16]{1,0:T(8,128)}, u32[]{:S(2)}) %copy-start.1) | copy-done | bytes 408
  0.8 1.5 %shard_map.37 = (f32[7,16,128]{2,1,0:T(8,128)S(1)}, f32[7,16,128]{2,1,0:T(8,128)S(1)}, s32[64,512]{1,0:T(8,128)S(1)}, f32[6,16]{1,0:T(8,128)S(1)}) custom-call(f32[6,64,512]{2,1,0:T(8,128)} %state_ref.3, s32[64,512]{1,0:T(8,128)} %grade_hbm.1, f32[6,16]{1,0:T(8,128)S(1)} %copy-done.1), custom_call_target="tpu_custom_call" | custom-call | flops 100000 | bytes 1000000 | tf_op jit(solution)/shard_map/pallas_call | solution.py:499
  2.3 2.2 %collective-permute-start = (f32[7,16,128]{2,1,0:T(8,128)S(1)}, f32[7,16,128]{2,1,0:T(8,128)S(1)}, u32[]{:S(2)}, u32[]{:S(2)}) collective-permute-start(f32[7,16,128]{2,1,0:T(8,128)S(1)} %get-tuple-element.22), channel_id=1, source_target_pairs={{0,1},{1,2},{2,3},{3,4},{4,5},{5,6},{6,7},{7,0},{8,9},{9,10},{10,1... | collective-permute-start | bytes 172040 | tf_op jit(solution)/shard_map/ppermute | solution.py:512
  4.4 0.0 collective-permute-start.1
  4.4 0.0 copy-done
  4.4 3.2 %shard_map.38 = (f32[6,4,80,128]{3,2,1,0:T(8,128)S(1)}, f32[8,4,80,128]{3,2,1,0:T(8,128)S(1)}, f32[6,4,32,128]{3,2,1,0:T(8,128)S(1)}, f32[4,4,24,128]{3,2,1,0:T(8,128)S(1)}) custom-call(f32[6,16]{1,0:T(8,128)S(1)} %get-tuple-element.20.table_ref, f32[6,64,512]{2,1,0:T(8,128)S(1)} %copy-done, s32[64,512]{1,0:T(8,128)S(1)} %get-tuple-element.21.grade_ref), custom_call_target="tpu_custom_call" | custom-call | flops 100000000 | bytes 10000000 | tf_op jit(solution)/shard_map/pallas_call | solution.py:515
  7.6 0.0 collective-permute-done.from_left_ref
  7.6 3.1 %collective-permute-done.1.from_right_ref = f32[7,16,128]{2,1,0:T(8,128)S(1)} collective-permute-done((f32[7,16,128]{2,1,0:T(8,128)S(1)}, f32[7,16,128]{2,1,0:T(8,128)S(1)}, u32[]{:S(2)}, u32[]{:S(2)}) %collective-permute-start.1) | collective-permute-done | bytes 57376 | tf_op jit(solution)/shard_map/ppermute | solution.py:513
  10.7 0.3 shard_map.39
  11.0 0.1 collective-permute-start.2
  11.1 5.3 %collective-permute-start.3 = (f32[7,5,24,128]{3,2,1,0:T(8,128)S(1)}, f32[7,5,24,128]{3,2,1,0:T(8,128)S(1)}, u32[]{:S(2)}, u32[]{:S(2)}) collective-permute-start(f32[7,5,24,128]{3,2,1,0:T(8,128)S(1)} %get-tuple-element.34), channel_id=1, source_target_pairs={{0,248},{8,0},{16,8},{24,16},{32,24},{40,32},{48,40},{56,48},{64,5... | collective-permute-start | bytes 1290248 | tf_op jit(solution)/shard_map/ppermute | solution.py:537
  16.5 6.3 %shard_map.40 = (f32[6,5,40,128]{3,2,1,0:T(8,128)S(1)}, f32[6,5,32,128]{3,2,1,0:T(8,128)S(1)}, f32[4,5,24,128]{3,2,1,0:T(8,128)S(1)}, f32[8,80,128]{2,1,0:T(8,128)S(1)}) custom-call(s32[1]{0:T(128)} %bitcast.gy_ref, f32[6,16]{1,0:T(8,128)S(1)} %get-tuple-element.20.table_ref, f32[7,64,128]{2,1,0:T(8,128)S(1)} %get-tuple-element.25.edge_ref, ...), custom_call_target="tpu_custom_call" | custom-call | flops 100000000 | bytes 10000000 | tf_op jit(solution)/shard_map/pallas_call | solution.py:538
  22.7 0.0 collective-permute-done.2.top_ref
  22.7 0.0 collective-permute-done.3.bottom_ref
  22.7 10.2 %shard_map.41 = f32[6,64,512]{2,1,0:T(8,128)} custom-call(s32[1]{0:T(128)} %bitcast.gy_ref, f32[6,16]{1,0:T(8,128)S(1)} %get-tuple-element.20.table_ref, s32[64,512]{1,0:T(8,128)S(1)} %get-tuple-element.21.grade_ref, f32[7,64,128]{2,1,0:T(8,128)S(1)} %get-tuple-element.25.edge_ref, f32[6,5,40,128]{3,2,1,0:T(8,128)S(1)} %get-tuple-element.29.keep_ref, ...), custom_call_target="tpu_custom_call" | custom-call | flops 100000000 | bytes 10000000 | tf_op jit(solution)/shard_map/pallas_call | solution.py:556
Async XLA Ops:
  0.0 4.4 %copy-start = (f32[6,64,512]{2,1,0:T(8,128)S(1)}, f32[6,64,512]{2,1,0:T(8,128)}, u32[]{:S(2)}) copy-start(f32[6,64,512]{2,1,0:T(8,128)} %state_ref.3) | copy-start | bytes 2359300
  0.0 0.8 %copy-start.1 = (f32[6,16]{1,0:T(8,128)S(1)}, f32[6,16]{1,0:T(8,128)}, u32[]{:S(2)}) copy-start(f32[6,16]{1,0:T(8,128)} %table_hbm.1) | copy-start | bytes 1156
  2.3 5.4 %collective-permute-start = (f32[7,16,128]{2,1,0:T(8,128)S(1)}, f32[7,16,128]{2,1,0:T(8,128)S(1)}, u32[]{:S(2)}, u32[]{:S(2)}) collective-permute-start(f32[7,16,128]{2,1,0:T(8,128)S(1)} %get-tuple-element.22), channel_id=1, source_target_pairs={{0,1},{1,2},{2,3},{3,4},{4,5},{5,6},{6,7},{7,0},{8,9},{9,10},{10,1... | collective-permute-start | bytes 172040 | tf_op jit(solution)/shard_map/ppermute | solution.py:512
  4.4 6.3 %collective-permute-start.1 = (f32[7,16,128]{2,1,0:T(8,128)S(1)}, f32[7,16,128]{2,1,0:T(8,128)S(1)}, u32[]{:S(2)}, u32[]{:S(2)}) collective-permute-start(f32[7,16,128]{2,1,0:T(8,128)S(1)} %get-tuple-element.23), channel_id=1, source_target_pairs={{0,7},{1,0},{2,1},{3,2},{4,3},{5,4},{6,5},{7,6},{8,15},{9,8},{10,9... | collective-permute-start | bytes 172040 | tf_op jit(solution)/shard_map/ppermute | solution.py:513
  11.0 11.7 %collective-permute-start.2 = (f32[7,5,24,128]{3,2,1,0:T(8,128)S(1)}, f32[7,5,24,128]{3,2,1,0:T(8,128)S(1)}, u32[]{:S(2)}, u32[]{:S(2)}) collective-permute-start(f32[7,5,24,128]{3,2,1,0:T(8,128)S(1)} %get-tuple-element.33), channel_id=1, source_target_pairs={{0,8},{8,16},{16,24},{24,32},{32,40},{40,48},{48,56},{56,64},{64,7... | collective-permute-start | bytes 1290248 | tf_op jit(solution)/shard_map/ppermute | solution.py:536
  11.1 11.6 %collective-permute-start.3 = (f32[7,5,24,128]{3,2,1,0:T(8,128)S(1)}, f32[7,5,24,128]{3,2,1,0:T(8,128)S(1)}, u32[]{:S(2)}, u32[]{:S(2)}) collective-permute-start(f32[7,5,24,128]{3,2,1,0:T(8,128)S(1)} %get-tuple-element.34), channel_id=1, source_target_pairs={{0,248},{8,0},{16,8},{24,16},{32,24},{40,32},{48,40},{56,48},{64,5... | collective-permute-start | bytes 1290248 | tf_op jit(solution)/shard_map/ppermute | solution.py:537
